TPU v7x, 32 devices: a whole 2x2x4 slice. The times are simulated.
32 devices in a mesh: gx: 2 (over x), gy: 8 (over z, y), lev: 2 (over core).
Axes of the slice: x: 2, y: 2, z: 4, core: 2. Of those that a mesh axis runs over, the one named last changes fastest.
Arguments:
- source: float32 [32, 256, 256], P('lev', 'gy', 'gx'), may hold values from -6 to 6
- remap_weights: float32 [512, 4, 128, 128], P(('gx', 'gy'))
- intersection_devices: int32 [512, 4], replicated, may hold values from 0 to 15, all different within a row; in each aligned block of 32 rows (0 to 31, 32 to 63, ...) at most 16 rows name the same one
- intersection_rows: int32 [512, 4], replicated, may hold values from 0 to 31
- smoothing: float32 [64, 1024], P('gx', 'gy'), may hold values from 0.04 to 0.24
Outputs:
- face_field: float32 [32, 64, 1024], P('lev', 'gx', 'gy')
Inputs may be any that keep to these rules, and one draw needn't show every extreme that they name: `intersection_devices`: each row names 4 different source tiles. Among the rows of one destination device (32 aligned rows), no source tile is named more than 16 times, and in every draw some source tile is named exactly 16 times.
All inputs are finite; a program needn't handle non-finite values.
Results may differ from a plain program's by a relative error of at most 0.00011.
Values sent between devices are 32-bit elements; how exact they have to be, the bound alone decides.
A program may use at most 64 MiB of HBM per device.

v0:
```python
import jax
import jax.numpy as jnp
from jax import lax
from jax.sharding import PartitionSpec as P

PASSES = 3


def padded_2(block, sides, width):
    for axis, dim in sides:
        count = lax.axis_size(axis)
        forward = [(i, i + 1) for i in range(count - 1)]
        backward = [(target, source) for source, target in forward]
        low = lax.ppermute(
            lax.slice_in_dim(block, block.shape[dim] - width, None, axis=dim), axis, forward
        )
        high = lax.ppermute(lax.slice_in_dim(block, 0, width, axis=dim), axis, backward)
        block = jnp.concatenate([low, block, high], axis=dim)
    return block


def ranks(entries):
    same = entries[:, :, None] == entries[:, None, :]
    order = jnp.arange(entries.shape[1])
    before = order[None, :] < order[:, None]
    return jnp.sum(jnp.logical_and(same, before[None]), axis=2)


def smooth_step(values, gained):
    laplace = (
        values[:, 2:, 1:-1]
        + values[:, :-2, 1:-1]
        + values[:, 1:-1, 2:]
        + values[:, 1:-1, :-2]
        - 4.0 * values[:, 1:-1, 1:-1]
    )
    return values[:, 1:-1, 1:-1] + gained * laplace


def shards(source, remap_weights, intersection_devices, intersection_rows, smoothing):
    along_x = lax.axis_size("gx")
    along_y = lax.axis_size("gy")
    devices = along_x * along_y
    frows = remap_weights.shape[0]
    fanin = remap_weights.shape[1]
    block = remap_weights.shape[2]
    capacity = 2 * max(1, frows * fanin // devices)
    myself = lax.axis_index("gx") * along_y + lax.axis_index("gy")
    entries = intersection_devices.reshape(devices, frows * fanin)
    slots = ranks(entries)
    lat_all = intersection_rows.reshape(devices, frows * fanin)
    hits = entries == myself
    slot_ids = jnp.arange(capacity, dtype=jnp.int32)
    matched = jnp.logical_and(hits[:, None, :], slots[:, None, :] == slot_ids[None, :, None])
    send_row = jnp.sum(jnp.where(matched, lat_all[:, None, :], 0), axis=2).reshape(
        devices * capacity
    )
    outgoing = jnp.take(source, send_row, axis=1)
    mine_entries = lax.dynamic_index_in_dim(entries, myself, 0, keepdims=False)
    mine_slots = lax.dynamic_index_in_dim(slots, myself, 0, keepdims=False)
    pick_slot = mine_entries * capacity + mine_slots
    incoming = lax.all_to_all(outgoing, ("gx", "gy"), split_axis=1, concat_axis=1, tiled=True)
    picked = jnp.take(incoming, pick_slot, axis=1).reshape(incoming.shape[0], frows, fanin, block)
    field = jnp.einsum("likc,ikcd->lid", picked, remap_weights, precision=lax.Precision.HIGHEST)
    for _ in range(PASSES):
        padded = padded_2(field, (("gx", 1), ("gy", 2)), 1)
        field = smooth_step(padded, smoothing)
    return field


def solution(mesh):
    return jax.shard_map(
        shards,
        mesh=mesh,
        in_specs=(P("lev", "gy", "gx"), P(("gx", "gy"), None, None, None), P(), P(), P("gx", "gy")),
        out_specs=P("lev", "gx", "gy"),
        check_vma=False,
    )
```

profile of v0, /device:TPU:0, one launch (start us, length us, event | category | flops | bytes accessed | tf_op | source)
XLA Modules:
  0.0 145.7 jit_solution(10208879844858102599)
XLA Ops:
  0.0 0.9 copy.16
  0.9 0.2 reshape.112
  1.1 0.6 convert_reduce_fusion
  1.7 0.8 copy.17
  2.6 0.2 broadcast_in_dim.44
  2.7 0.3 select_reduce_fusion
  3.1 0.1 reshape.114
  3.2 0.1 reshape.113
  3.3 5.0 %gather_fusion = f32[256,16,128]{2,0,1:T(8,128)S(1)} fusion(f32[16,32,128]{2,1,0:T(8,128)S(1)} %copy-done, s32[1024]{0:T(1024)S(1)} %pad_clamp_fusion.1), kind=kCustom, calls=%fused_computation | custom fusion | bytes 4195328 | tf_op jit(solution)/shard_map/jit(_take)/gather | solution.py:58
  8.3 0.3 select_bitcast_fusion
  8.6 2.6 %copy.18 = f32[16,256,128]{2,0,1:T(8,128)} copy(f32[16,256,128]{2,1,0:T(8,128)S(1)} %select_bitcast_fusion) | data formatting | bytes 4194304 | tf_op jit(solution)/shard_map/jit(_take)/select_n | solution.py:58
  11.2 8.3 %all-to-all-start = ((f32[16,256,128]{2,0,1:T(8,128)}), f32[16,256,128]{2,0,1:T(8,128)S(1)}, u32[]{:S(2)}, u32[]{:S(2)}) async-start(f32[16,256,128]{2,0,1:T(8,128)} %copy.18), calls=%async_computation | async-start | bytes 4194304 | tf_op jit(solution)/shard_map/all_to_all | solution.py:62
  19.5 0.5 broadcast.102
  20.0 0.7 fusion.24
  20.7 0.1 add.109
  20.8 45.9 %all-to-all-done = f32[16,256,128]{2,0,1:T(8,128)S(1)} async-done(((f32[16,256,128]{2,0,1:T(8,128)}), f32[16,256,128]{2,0,1:T(8,128)S(1)}, u32[]{:S(2)}, u32[]{:S(2)}) %all-to-all-start) | async-done | bytes 2097184 | tf_op jit(solution)/shard_map/all_to_all | solution.py:62
  66.7 0.8 gather_fusion.1
  67.5 6.6 %convolution_bitcast_fusion = f32[16,32,128]{2,0,1:T(8,128)S(1)} fusion(f32[32,4,128,128]{3,2,1,0:T(8,128)} %param.6, f32[16,32,4,128]{3,0,2,1:T(8,128)S(1)} %bitcast.16, pred[32,4]{1,0:T(8,128)(4,1)S(1)} %compare_and_fusion), kind=kOutput, calls=%fused_computation.3 | convolution fusion | flops 402915328 | bytes 9699456 | tf_op jit(solution)/shard_map/likc,ikcd->lid/dot_general | solution.py:64
  74.2 3.4 %collective-permute-start.1 = (f32[16,1,128]{2,0,1:T(8,128)S(1)}, f32[16,1,128]{2,0,1:T(8,128)S(1)}, u32[]{:S(2)}, u32[]{:S(2)}) collective-permute-start(f32[16,1,128]{2,0,1:T(8,128)S(1)} %get-tuple-element.17), channel_id=1, source_target_pairs={{0,16},{1,17},{2,18},{3,19},{4,20},{5,21},{6,22},{7,23},{8,24},{9,... | collective-permute-start | bytes 24584 | tf_op jit(solution)/shard_map/ppermute | solution.py:14
  77.5 1.3 collective-permute-start
  78.8 0.0 collective-permute-done.1
  78.9 4.2 %collective-permute-done = f32[16,1,128]{2,0,1:T(8,128)S(1)} collective-permute-done((f32[16,1,128]{2,0,1:T(8,128)S(1)}, f32[16,1,128]{2,0,1:T(8,128)S(1)}, u32[]{:S(2)}, u32[]{:S(2)}) %collective-permute-start) | collective-permute-done | bytes 8224 | tf_op jit(solution)/shard_map/ppermute | solution.py:17
  83.1 0.1 fusion.27
  83.3 1.3 collective-permute-start.2
  84.6 4.6 %collective-permute-start.3 = (f32[16,34,1]{2,0,1:T(8,128)S(1)}, f32[16,34,1]{2,0,1:T(8,128)S(1)}, u32[]{:S(2)}, u32[]{:S(2)}) collective-permute-start(f32[16,34,1]{2,0,1:T(8,128)S(1)} %get-tuple-element.12), channel_id=1, source_target_pairs={{0,2},{2,4},{4,6},{6,8},{8,10},{10,12},{12,14},{1,3},{3,5},{5,7},{... | collective-permute-start | bytes 6536 | tf_op jit(solution)/shard_map/ppermute | solution.py:14
  89.1 2.6 %collective-permute-done.2 = f32[16,34,1]{2,0,1:T(8,128)S(1)} collective-permute-done((f32[16,34,1]{2,0,1:T(8,128)S(1)}, f32[16,34,1]{2,0,1:T(8,128)S(1)}, u32[]{:S(2)}, u32[]{:S(2)}) %collective-permute-start.2) | collective-permute-done | bytes 2208 | tf_op jit(solution)/shard_map/ppermute | solution.py:17
  91.7 5.2 %collective-permute-done.3 = f32[16,34,1]{2,0,1:T(8,128)S(1)} collective-permute-done((f32[16,34,1]{2,0,1:T(8,128)S(1)}, f32[16,34,1]{2,0,1:T(8,128)S(1)}, u32[]{:S(2)}, u32[]{:S(2)}) %collective-permute-start.3) | collective-permute-done | bytes 2208 | tf_op jit(solution)/shard_map/ppermute | solution.py:14
  96.9 0.3 fusion.18
  97.2 1.9 %collective-permute-start.5 = (f32[16,1,128]{2,0,1:T(8,128)S(1)}, f32[16,1,128]{2,0,1:T(8,128)S(1)}, u32[]{:S(2)}, u32[]{:S(2)}) collective-permute-start(f32[16,1,128]{2,0,1:T(8,128)S(1)} %get-tuple-element.15), channel_id=1, source_target_pairs={{0,16},{1,17},{2,18},{3,19},{4,20},{5,21},{6,22},{7,23},{8,24},{9,... | collective-permute-start | bytes 24584 | tf_op jit(solution)/shard_map/ppermute | solution.py:14
  99.1 1.3 collective-permute-start.4
  100.4 0.0 collective-permute-done.5
  100.5 4.2 %collective-permute-done.4 = f32[16,1,128]{2,0,1:T(8,128)S(1)} collective-permute-done((f32[16,1,128]{2,0,1:T(8,128)S(1)}, f32[16,1,128]{2,0,1:T(8,128)S(1)}, u32[]{:S(2)}, u32[]{:S(2)}) %collective-permute-start.4) | collective-permute-done | bytes 8224 | tf_op jit(solution)/shard_map/ppermute | solution.py:17
  104.7 0.1 fusion.26
  104.8 1.3 collective-permute-start.6
  106.1 5.0 %collective-permute-start.7 = (f32[16,34,1]{2,0,1:T(8,128)S(1)}, f32[16,34,1]{2,0,1:T(8,128)S(1)}, u32[]{:S(2)}, u32[]{:S(2)}) collective-permute-start(f32[16,34,1]{2,0,1:T(8,128)S(1)} %get-tuple-element.10), channel_id=1, source_target_pairs={{0,2},{2,4},{4,6},{6,8},{8,10},{10,12},{12,14},{1,3},{3,5},{5,7},{... | collective-permute-start | bytes 6536 | tf_op jit(solution)/shard_map/ppermute | solution.py:14
  111.2 3.5 %collective-permute-done.6 = f32[16,34,1]{2,0,1:T(8,128)S(1)} collective-permute-done((f32[16,34,1]{2,0,1:T(8,128)S(1)}, f32[16,34,1]{2,0,1:T(8,128)S(1)}, u32[]{:S(2)}, u32[]{:S(2)}) %collective-permute-start.6) | collective-permute-done | bytes 2208 | tf_op jit(solution)/shard_map/ppermute | solution.py:17
  114.6 6.1 %collective-permute-done.7 = f32[16,34,1]{2,0,1:T(8,128)S(1)} collective-permute-done((f32[16,34,1]{2,0,1:T(8,128)S(1)}, f32[16,34,1]{2,0,1:T(8,128)S(1)}, u32[]{:S(2)}, u32[]{:S(2)}) %collective-permute-start.7) | collective-permute-done | bytes 2208 | tf_op jit(solution)/shard_map/ppermute | solution.py:14
  120.7 0.3 fusion.12
  121.0 1.9 %collective-permute-start.9 = (f32[16,1,128]{2,0,1:T(8,128)S(1)}, f32[16,1,128]{2,0,1:T(8,128)S(1)}, u32[]{:S(2)}, u32[]{:S(2)}) collective-permute-start(f32[16,1,128]{2,0,1:T(8,128)S(1)} %get-tuple-element.13), channel_id=1, source_target_pairs={{0,16},{1,17},{2,18},{3,19},{4,20},{5,21},{6,22},{7,23},{8,24},{9,... | collective-permute-start | bytes 24584 | tf_op jit(solution)/shard_map/ppermute | solution.py:14
  123.0 1.3 collective-permute-start.8
  124.3 4.2 %collective-permute-done.8 = f32[16,1,128]{2,0,1:T(8,128)S(1)} collective-permute-done((f32[16,1,128]{2,0,1:T(8,128)S(1)}, f32[16,1,128]{2,0,1:T(8,128)S(1)}, u32[]{:S(2)}, u32[]{:S(2)}) %collective-permute-start.8) | collective-permute-done | bytes 8224 | tf_op jit(solution)/shard_map/ppermute | solution.py:17
  128.6 0.1 fusion.25
  128.7 1.3 collective-permute-start.10
  130.0 5.0 %collective-permute-start.11 = (f32[16,34,1]{2,0,1:T(8,128)S(1)}, f32[16,34,1]{2,0,1:T(8,128)S(1)}, u32[]{:S(2)}, u32[]{:S(2)}) collective-permute-start(f32[16,34,1]{2,0,1:T(8,128)S(1)} %get-tuple-element.8), channel_id=1, source_target_pairs={{0,2},{2,4},{4,6},{6,8},{8,10},{10,12},{12,14},{1,3},{3,5},{5,7},{... | collective-permute-start | bytes 6536 | tf_op jit(solution)/shard_map/ppermute | solution.py:14
  135.0 3.5 %collective-permute-done.10 = f32[16,34,1]{2,0,1:T(8,128)S(1)} collective-permute-done((f32[16,34,1]{2,0,1:T(8,128)S(1)}, f32[16,34,1]{2,0,1:T(8,128)S(1)}, u32[]{:S(2)}, u32[]{:S(2)}) %collective-permute-start.10) | collective-permute-done | bytes 2208 | tf_op jit(solution)/shard_map/ppermute | solution.py:17
  138.5 6.1 %collective-permute-done.11 = f32[16,34,1]{2,0,1:T(8,128)S(1)} collective-permute-done((f32[16,34,1]{2,0,1:T(8,128)S(1)}, f32[16,34,1]{2,0,1:T(8,128)S(1)}, u32[]{:S(2)}, u32[]{:S(2)}) %collective-permute-start.11) | collective-permute-done | bytes 2208 | tf_op jit(solution)/shard_map/ppermute | solution.py:14
  144.6 0.3 fusion.6
  144.9 0.8 copy.19
  (19 shorter events, 0.2 us)
Async XLA Ops:
  0.0 3.3 %copy-start = (f32[16,32,128]{2,1,0:T(8,128)S(1)}, f32[16,32,128]{2,1,0:T(8,128)}, u32[]{:S(2)}) copy-start(f32[16,32,128]{2,1,0:T(8,128)} %param.5) | copy-start | bytes 786436
  11.2 55.6 %all-to-all-start = ((f32[16,256,128]{2,0,1:T(8,128)}), f32[16,256,128]{2,0,1:T(8,128)S(1)}, u32[]{:S(2)}, u32[]{:S(2)}) async-start(f32[16,256,128]{2,0,1:T(8,128)} %copy.18), calls=%async_computation | async-start | bytes 4194304 | tf_op jit(solution)/shard_map/all_to_all | solution.py:62
  67.5 29.4 %copy-start.1 = (f32[32,128]{1,0:T(8,128)S(1)}, f32[32,128]{1,0:T(8,128)}, u32[]{:S(2)}) copy-start(f32[32,128]{1,0:T(8,128)} %param.9) | copy-start | bytes 49156
  74.2 4.7 %collective-permute-start.1 = (f32[16,1,128]{2,0,1:T(8,128)S(1)}, f32[16,1,128]{2,0,1:T(8,128)S(1)}, u32[]{:S(2)}, u32[]{:S(2)}) collective-permute-start(f32[16,1,128]{2,0,1:T(8,128)S(1)} %get-tuple-element.17), channel_id=1, source_target_pairs={{0,16},{1,17},{2,18},{3,19},{4,20},{5,21},{6,22},{7,23},{8,24},{9,... | collective-permute-start | bytes 24584 | tf_op jit(solution)/shard_map/ppermute | solution.py:14
  77.5 5.5 %collective-permute-start = (f32[16,1,128]{2,0,1:T(8,128)S(1)}, f32[16,1,128]{2,0,1:T(8,128)S(1)}, u32[]{:S(2)}, u32[]{:S(2)}) collective-permute-start(f32[16,1,128]{2,0,1:T(8,128)S(1)} %get-tuple-element.18), channel_id=1, source_target_pairs={{16,0},{17,1},{18,2},{19,3},{20,4},{21,5},{22,6},{23,7},{24,8},{25... | collective-permute-start | bytes 24584 | tf_op jit(solution)/shard_map/ppermute | solution.py:17
  83.3 8.4 %collective-permute-start.2 = (f32[16,34,1]{2,0,1:T(8,128)S(1)}, f32[16,34,1]{2,0,1:T(8,128)S(1)}, u32[]{:S(2)}, u32[]{:S(2)}) collective-permute-start(f32[16,34,1]{2,0,1:T(8,128)S(1)} %get-tuple-element.11), channel_id=1, source_target_pairs={{2,0},{4,2},{6,4},{8,6},{10,8},{12,10},{14,12},{3,1},{5,3},{7,5},{... | collective-permute-start | bytes 6536 | tf_op jit(solution)/shard_map/ppermute | solution.py:17
  84.6 12.3 %collective-permute-start.3 = (f32[16,34,1]{2,0,1:T(8,128)S(1)}, f32[16,34,1]{2,0,1:T(8,128)S(1)}, u32[]{:S(2)}, u32[]{:S(2)}) collective-permute-start(f32[16,34,1]{2,0,1:T(8,128)S(1)} %get-tuple-element.12), channel_id=1, source_target_pairs={{0,2},{2,4},{4,6},{6,8},{8,10},{10,12},{12,14},{1,3},{3,5},{5,7},{... | collective-permute-start | bytes 6536 | tf_op jit(solution)/shard_map/ppermute | solution.py:14
  97.2 3.3 %collective-permute-start.5 = (f32[16,1,128]{2,0,1:T(8,128)S(1)}, f32[16,1,128]{2,0,1:T(8,128)S(1)}, u32[]{:S(2)}, u32[]{:S(2)}) collective-permute-start(f32[16,1,128]{2,0,1:T(8,128)S(1)} %get-tuple-element.15), channel_id=1, source_target_pairs={{0,16},{1,17},{2,18},{3,19},{4,20},{5,21},{6,22},{7,23},{8,24},{9,... | collective-permute-start | bytes 24584 | tf_op jit(solution)/shard_map/ppermute | solution.py:14
  99.1 5.5 %collective-permute-start.4 = (f32[16,1,128]{2,0,1:T(8,128)S(1)}, f32[16,1,128]{2,0,1:T(8,128)S(1)}, u32[]{:S(2)}, u32[]{:S(2)}) collective-permute-start(f32[16,1,128]{2,0,1:T(8,128)S(1)} %get-tuple-element.16), channel_id=1, source_target_pairs={{16,0},{17,1},{18,2},{19,3},{20,4},{21,5},{22,6},{23,7},{24,8},{25... | collective-permute-start | bytes 24584 | tf_op jit(solution)/shard_map/ppermute | solution.py:17
  104.8 9.8 %collective-permute-start.6 = (f32[16,34,1]{2,0,1:T(8,128)S(1)}, f32[16,34,1]{2,0,1:T(8,128)S(1)}, u32[]{:S(2)}, u32[]{:S(2)}) collective-permute-start(f32[16,34,1]{2,0,1:T(8,128)S(1)} %get-tuple-element.9), channel_id=1, source_target_pairs={{2,0},{4,2},{6,4},{8,6},{10,8},{12,10},{14,12},{3,1},{5,3},{7,5},{... | collective-permute-start | bytes 6536 | tf_op jit(solution)/shard_map/ppermute | solution.py:17
  106.1 14.6 %collective-permute-start.7 = (f32[16,34,1]{2,0,1:T(8,128)S(1)}, f32[16,34,1]{2,0,1:T(8,128)S(1)}, u32[]{:S(2)}, u32[]{:S(2)}) collective-permute-start(f32[16,34,1]{2,0,1:T(8,128)S(1)} %get-tuple-element.10), channel_id=1, source_target_pairs={{0,2},{2,4},{4,6},{6,8},{8,10},{10,12},{12,14},{1,3},{3,5},{5,7},{... | collective-permute-start | bytes 6536 | tf_op jit(solution)/shard_map/ppermute | solution.py:14
  121.0 3.3 %collective-permute-start.9 = (f32[16,1,128]{2,0,1:T(8,128)S(1)}, f32[16,1,128]{2,0,1:T(8,128)S(1)}, u32[]{:S(2)}, u32[]{:S(2)}) collective-permute-start(f32[16,1,128]{2,0,1:T(8,128)S(1)} %get-tuple-element.13), channel_id=1, source_target_pairs={{0,16},{1,17},{2,18},{3,19},{4,20},{5,21},{6,22},{7,23},{8,24},{9,... | collective-permute-start | bytes 24584 | tf_op jit(solution)/shard_map/ppermute | solution.py:14
  123.0 5.5 %collective-permute-start.8 = (f32[16,1,128]{2,0,1:T(8,128)S(1)}, f32[16,1,128]{2,0,1:T(8,128)S(1)}, u32[]{:S(2)}, u32[]{:S(2)}) collective-permute-start(f32[16,1,128]{2,0,1:T(8,128)S(1)} %get-tuple-element.14), channel_id=1, source_target_pairs={{16,0},{17,1},{18,2},{19,3},{20,4},{21,5},{22,6},{23,7},{24,8},{25... | collective-permute-start | bytes 24584 | tf_op jit(solution)/shard_map/ppermute | solution.py:17
  128.7 9.8 %collective-permute-start.10 = (f32[16,34,1]{2,0,1:T(8,128)S(1)}, f32[16,34,1]{2,0,1:T(8,128)S(1)}, u32[]{:S(2)}, u32[]{:S(2)}) collective-permute-start(f32[16,34,1]{2,0,1:T(8,128)S(1)} %get-tuple-element.7), channel_id=1, source_target_pairs={{2,0},{4,2},{6,4},{8,6},{10,8},{12,10},{14,12},{3,1},{5,3},{7,5},{... | collective-permute-start | bytes 6536 | tf_op jit(solution)/shard_map/ppermute | solution.py:17
  130.0 14.6 %collective-permute-start.11 = (f32[16,34,1]{2,0,1:T(8,128)S(1)}, f32[16,34,1]{2,0,1:T(8,128)S(1)}, u32[]{:S(2)}, u32[]{:S(2)}) collective-permute-start(f32[16,34,1]{2,0,1:T(8,128)S(1)} %get-tuple-element.8), channel_id=1, source_target_pairs={{0,2},{2,4},{4,6},{6,8},{8,10},{10,12},{12,14},{1,3},{3,5},{5,7},{... | collective-permute-start | bytes 6536 | tf_op jit(solution)/shard_map/ppermute | solution.py:14
where the time goes:
time: 146 us
  waiting for transfers between devices  85.5 us (59%)
  starting transfers between devices  37.9 us (26%)
  local copies, waits for them, and re-layouts  12.3 us (8%)
  matrix products  6.64 us (5%)
  other arithmetic  2.91 us (2%)
    all_to_all x1, waiting for transfers between devices, shards(): lax.all_to_all(outgoing, ('gx', 'gy'), split_axis=1, concat_axis=1, tiled...  45.9 us
    ppermute x6, waiting for transfers between devices, padded_2(): lax.ppermute(lax.slice_in_dim(block, 0, width, axis=dim), axis, backward)  22.1 us
    ppermute x6, starting transfers between devices, padded_2(): lax.ppermute(lax.slice_in_dim(block, block.shape[dim] - width, None, axis...  21.9 us
    ppermute x6, waiting for transfers between devices, padded_2(): lax.ppermute(lax.slice_in_dim(block, block.shape[dim] - width, None, axis...  17.6 us
    all_to_all x1, starting transfers between devices, shards(): lax.all_to_all(outgoing, ('gx', 'gy'), split_axis=1, concat_axis=1, tiled...  8.31 us
    ppermute x6, starting transfers between devices, padded_2(): lax.ppermute(lax.slice_in_dim(block, 0, width, axis=dim), axis, backward)  7.75 us
    dot_general x1, matrix products, shards(): jnp.einsum('likc,ikcd->lid', picked, remap_weights, precision=lax.Precisi...  6.64 us
    gather x1, local copies, waits for them, and re-layouts, shards(): outgoing = jnp.take(source, send_row, axis=1)  4.97 us
  transfers between devices with their start and end apart: 13, of which 10 were waited for; matrix products, arithmetic and copies ran while one was open for 1% of the time, Pallas kernels for 0%

commit v1 on v0

v1 whole, which is shorter than its diff:
```python
import functools

import jax
import jax.numpy as jnp
from jax import lax
from jax.experimental import pallas as pl
from jax.experimental.pallas import tpu as pltpu
from jax.sharding import PartitionSpec as P

PASSES = 3
MESH = pl.DeviceIdType.MESH
DIRS = [(dx, dy) for dx in (-1, 0, 1) for dy in (-1, 0, 1) if (dx, dy) != (0, 0)]
OPPOSITE = [DIRS.index((-dx, -dy)) for dx, dy in DIRS]
LANES = 128
STRIP = 8
PER_TILE = LANES // STRIP


def layout(along_x, along_y, capacity, rows):
    inner = 2 if along_y % 2 == 0 else 1
    if capacity * inner * along_x > rows:
        return along_y // inner, inner
    return 1, along_y


def kernel(dims, send_rows, pick, src, weights, smooth, out, inbox, outbox, w_full, w_high, w_low,
           main_a, main_b, side_a, side_b, s_main, s_side, s_in, edge, edge_in,
           send_sem, recv_sem, chain_send, chain_recv, s_send, s_recv, h_send, h_recv, w_sem, *chain):
    along_x, along_y, depth, inner, capacity = dims
    frows, fan = w_full.shape[0], pick.shape[0] // w_full.shape[0]
    levels = src.shape[1]
    columns = along_x * inner
    ups, downs = chain[: depth - 1], chain[depth - 1:]
    x, y, lev = lax.axis_index("gx"), lax.axis_index("gy"), lax.axis_index("lev")
    z, yi = y // inner, y % inner
    column = x * inner + yi
    lane = lax.broadcasted_iota(jnp.int32, (levels, LANES), 1)

    def column_id(c):
        return (c // inner, z * inner + c % inner, lev)

    def near(dx, dy):
        ok = jnp.logical_and(
            jnp.logical_and(x + dx >= 0, x + dx < along_x),
            jnp.logical_and(y + dy >= 0, y + dy < along_y),
        )
        return ok, (x + dx, y + dy, lev)

    barrier = pltpu.get_barrier_semaphore()

    def greet(device):
        pl.semaphore_signal(barrier, inc=1, device_id=device, device_id_type=MESH)

    def greet_column(q, carry):
        greet(column_id(lax.rem(column + q, columns)))
        return carry

    lax.fori_loop(1, columns, greet_column, 0)
    total = columns - 1
    links = [near(dx, dy) for dx, dy in DIRS]
    if depth > 1:
        links = links + [(z < depth - 1, (x, y + inner, lev)), (z > 0, (x, y - inner, lev))]
    for ok, device in links:
        total = total + ok.astype(jnp.int32)

        @pl.when(ok)
        def _():
            greet(device)

    w_copy = pltpu.make_async_copy(weights, w_full, w_sem)
    w_copy.start()
    pl.semaphore_wait(barrier, total)

    def chain_copy(up, t):
        source = src if t == 0 else (ups if up else downs)[t - 1]
        step = inner if up else -inner
        return pltpu.make_async_remote_copy(
            src_ref=source, dst_ref=(ups if up else downs)[t],
            send_sem=chain_send.at[0 if up else 1, t], recv_sem=chain_recv.at[0 if up else 1, t],
            device_id=(x, y + step, lev), device_id_type=MESH)

    def slot_copy(q, tile):
        c = lax.rem(column + q, columns)
        return pltpu.make_async_remote_copy(
            src_ref=outbox.at[pl.ds((c * depth + tile) * capacity, capacity)],
            dst_ref=inbox.at[pl.ds((column * depth + tile) * capacity, capacity)],
            send_sem=send_sem.at[q * depth + tile], recv_sem=recv_sem.at[q * depth + tile],
            device_id=column_id(c), device_id_type=MESH)

    def ship(chunk, tile):
        def peer(q, carry):
            base = (lax.rem(column + q, columns) * depth + tile) * capacity
            for j in range(capacity):
                outbox[base + j] = chunk[send_rows[base + j]]
            slot_copy(q, tile).start()
            return carry

        lax.fori_loop(1, columns, peer, 0)
        base = (column * depth + tile) * capacity
        for j in range(capacity):
            inbox[base + j] = chunk[send_rows[base + j]]

    if depth > 1:
        @pl.when(z < depth - 1)
        def _():
            chain_copy(True, 0).start()

        @pl.when(z > 0)
        def _():
            chain_copy(False, 0).start()

    ship(src, z)

    def s_copy(k):
        ok, device = near(*DIRS[k])
        return ok, pltpu.make_async_remote_copy(
            src_ref=smooth, dst_ref=s_in.at[OPPOSITE[k]], send_sem=s_send.at[k],
            recv_sem=s_recv.at[OPPOSITE[k]], device_id=device, device_id_type=MESH)

    def h_copy(k):
        dx, dy = DIRS[k]
        ok, device = near(dx, dy)
        if dy == 0:
            source = main_a.at[pl.ds(frows if dx > 0 else PASSES, PASSES)]
            target = main_a.at[pl.ds(0 if dx > 0 else frows + PASSES, PASSES)]
        else:
            source, target = edge, edge_in.at[OPPOSITE[k]]
        return ok, pltpu.make_async_remote_copy(
            src_ref=source, dst_ref=target, send_sem=h_send.at[k],
            recv_sem=h_recv.at[OPPOSITE[k]], device_id=device, device_id_type=MESH)

    def arrival(make, k):
        return make(OPPOSITE[k])[1]

    for k in range(len(DIRS)):
        ok, copy = s_copy(k)

        @pl.when(ok)
        def _():
            copy.start()

    for k, (dx, dy) in enumerate(DIRS):
        ok, _ = near(dx, dy)

        @pl.when(jnp.logical_not(ok))
        def _():
            s_in[k] = jnp.zeros(s_in.shape[1:], jnp.float32)
            if dy == 0:
                main_a[pl.ds(0 if dx < 0 else frows + PASSES, PASSES)] = jnp.zeros(
                    (PASSES,) + main_a.shape[1:], jnp.float32)
            else:
                edge_in[k] = jnp.zeros(edge_in.shape[1:], jnp.float32)

    for t in range(depth - 1):
        for up, ok, onward in ((True, z >= t + 1, z < depth - 1), (False, z + 1 + t <= depth - 1, z > 0)):
            @pl.when(ok)
            def _():
                chain_copy(up, t).wait_recv()
                if t + 1 < depth - 1:
                    @pl.when(onward)
                    def _():
                        chain_copy(up, t + 1).start()
                ship((ups if up else downs)[t], z - 1 - t if up else z + 1 + t)
        if t == 0:
            split_weights(w_copy, w_full, w_high, w_low)
    if depth == 1:
        split_weights(w_copy, w_full, w_high, w_low)

    for k in range(len(DIRS)):
        ok, copy = s_copy(k)

        @pl.when(ok)
        def _():
            copy.wait_send()
            arrival_wait(s_in.at[k], smooth, s_recv.at[k])

    row_lane = lax.broadcasted_iota(jnp.int32, (1, LANES), 1)

    def side(left, right):
        return jnp.where(row_lane < PASSES, right, jnp.where(row_lane >= LANES - PASSES, left, 0.0))

    at = {d: k for k, d in enumerate(DIRS)}
    for i in range(frows):
        s_main[PASSES + i] = smooth[i:i + 1, :]
        s_side[PASSES + i] = side(s_in[at[0, -1], i:i + 1, :], s_in[at[0, 1], i:i + 1, :])
    for i in range(PASSES):
        low, high = frows - PASSES + i, frows + PASSES + i
        s_main[i] = s_in[at[-1, 0], low:low + 1, :]
        s_side[i] = side(s_in[at[-1, -1], low:low + 1, :], s_in[at[-1, 1], low:low + 1, :])
        s_main[high] = s_in[at[1, 0], i:i + 1, :]
        s_side[high] = side(s_in[at[1, -1], i:i + 1, :], s_in[at[1, 1], i:i + 1, :])

    def landed(n, carry):
        slot_copy(n // depth, lax.rem(n, depth)).wait_recv()
        return carry

    lax.fori_loop(depth, columns * depth, landed, 0)

    def product(i):
        blocks = jnp.concatenate([inbox[pick[i * fan + k]] for k in range(fan)], axis=1)
        high = blocks.astype(jnp.bfloat16)
        low = (blocks - high.astype(jnp.float32)).astype(jnp.bfloat16)
        both = jnp.dot(jnp.concatenate([high, low], axis=0), w_high[i], preferred_element_type=jnp.float32)
        rest = jnp.dot(high, w_low[i], preferred_element_type=jnp.float32)
        main_a[PASSES + i] = both[:levels] + (both[levels:] + rest)

    def products(n, carry):
        for j in range(4):
            product(n * 4 + j)
        return carry

    lax.fori_loop(0, frows // 4, products, 0)

    for k, (dx, dy) in enumerate(DIRS):
        if dy == 0:
            ok, copy = h_copy(k)

            @pl.when(ok)
            def _():
                copy.start()

    tiles = frows // PER_TILE
    for b in range(tiles):
        packed = jnp.zeros((levels, LANES), jnp.float32)
        for j in range(PER_TILE):
            moved = pltpu.roll(main_a[PASSES + b * PER_TILE + j], STRIP * j + STRIP // 2, axis=1)
            packed = jnp.where(lane // STRIP == j, moved, packed)
        edge[b] = packed
    for k, (dx, dy) in enumerate(DIRS):
        if dy != 0:
            ok, copy = h_copy(k)

            @pl.when(ok)
            def _():
                copy.start()

    def sent(n, carry):
        slot_copy(n // depth, lax.rem(n, depth)).wait_send()
        return carry

    lax.fori_loop(depth, columns * depth, sent, 0)
    for t in range(depth - 1):
        @pl.when(jnp.logical_and(z < depth - 1, z - t >= 0))
        def _():
            chain_copy(True, t).wait_send()

        @pl.when(jnp.logical_and(z > 0, z + t <= depth - 1))
        def _():
            chain_copy(False, t).wait_send()

    for k, (dx, dy) in enumerate(DIRS):
        ok, copy = h_copy(k)

        @pl.when(ok)
        def _():
            copy.wait_send()
            if dy == 0:
                rows = main_a.at[pl.ds(0 if dx < 0 else frows + PASSES, PASSES)]
                arrival_wait(rows, rows, h_recv.at[k])
            else:
                arrival_wait(edge_in.at[k], edge, h_recv.at[k])

    inside = jnp.logical_or(lane < PASSES, lane >= LANES - PASSES)

    def unpack(row, tile, place, left, right):
        merged = jnp.where(lax.rem(lane, STRIP) < STRIP // 2, edge_in[left, tile], edge_in[right, tile])
        moved = pltpu.roll(merged, (2 * LANES - STRIP * place - STRIP // 2) % LANES, axis=1)
        side_a[row] = jnp.where(inside, moved, 0.0)

    for i in range(frows):
        unpack(PASSES + i, i // PER_TILE, i % PER_TILE, at[0, -1], at[0, 1])
    for i in range(PASSES):
        far = frows - PASSES + i
        unpack(i, far // PER_TILE, far % PER_TILE, at[-1, -1], at[-1, 1])
        unpack(frows + PASSES + i, 0, i, at[1, -1], at[1, 1])

    first, last = lane == 0, lane == LANES - 1

    def smooth_row(r, main, sides, write):
        u, h = main[r], sides[r]
        u_up, u_down = pltpu.roll(u, 1, axis=1), pltpu.roll(u, LANES - 1, axis=1)
        h_up, h_down = pltpu.roll(h, 1, axis=1), pltpu.roll(h, LANES - 1, axis=1)
        lap = (main[r + 1] + main[r - 1] + jnp.where(last, h_down, u_down)
               + jnp.where(first, h_up, u_up) - 4.0 * u)
        lap_h = (sides[r + 1] + sides[r - 1] + jnp.where(last, u_down, h_down)
                 + jnp.where(first, u_up, h_up) - 4.0 * h)
        write(r, u + s_main[r] * lap, h + s_side[r] * lap_h)

    def write_b(r, u, h):
        main_b[r] = u
        side_b[r] = h

    def write_a(r, u, h):
        main_a[r] = u
        side_a[r] = h

    def write_out(r, u, h):
        out[r - PASSES] = u

    for p, (main, sides, write) in enumerate((
            (main_a, side_a, write_b), (main_b, side_b, write_a), (main_a, side_a, write_out))):
        start, count = p + 1, frows + 2 * PASSES - 2 * (p + 1)
        chunk = 4 if count % 4 == 0 else 2

        def rows(n, carry):
            for j in range(chunk):
                smooth_row(start + n * chunk + j, main, sides, write)
            return carry

        lax.fori_loop(0, count // chunk, rows, 0)


def arrival_wait(target, source, sem):
    pltpu.make_async_copy(source, target, sem).wait()


def split_weights(w_copy, w_full, w_high, w_low):
    w_copy.wait()

    def one(i, carry):
        value = w_full[i]
        high = value.astype(jnp.bfloat16)
        w_high[i] = high
        w_low[i] = (value - high.astype(jnp.float32)).astype(jnp.bfloat16)
        return carry

    lax.fori_loop(0, w_full.shape[0], one, 0)


def shards(source, remap_weights, intersection_devices, intersection_rows, smoothing):
    along_x = lax.axis_size("gx")
    along_y = lax.axis_size("gy")
    devices = along_x * along_y
    frows, fanin, block = remap_weights.shape[:3]
    levels, srows = source.shape[:2]
    capacity = 2 * max(1, frows * fanin // devices)
    depth, inner = layout(along_x, along_y, capacity, srows)
    columns = along_x * inner
    x, y = lax.axis_index("gx"), lax.axis_index("gy")
    z, yi = y // inner, y % inner
    column = x * inner + yi

    def plane(table):
        table = table.reshape(along_x, depth, inner, frows, fanin)
        table = lax.dynamic_index_in_dim(table, z, 1, keepdims=False)
        return table.reshape(columns, frows * fanin)

    entries, lats = plane(intersection_devices), plane(intersection_rows)
    order = jnp.arange(frows * fanin)
    same = jnp.logical_and(entries[:, :, None] == entries[:, None, :], order[None, :] < order[:, None])
    slots = jnp.sum(same.astype(jnp.int32), axis=2)
    tiles = x * along_y + jnp.arange(depth) * inner + yi
    matched = jnp.logical_and(
        entries[:, None, None, :] == tiles[None, :, None, None],
        slots[:, None, None, :] == jnp.arange(capacity)[None, None, :, None])
    send_rows = jnp.sum(jnp.where(matched, lats[:, None, None, :], 0), axis=3).reshape(-1)
    mine = lax.dynamic_index_in_dim(entries, column, 0, keepdims=False)
    my_slots = lax.dynamic_index_in_dim(slots, column, 0, keepdims=False)
    my_y = mine % along_y
    pick = (((mine // along_y) * inner + my_y % inner) * depth + my_y // inner) * capacity + my_slots

    full = frows + 2 * PASSES
    vmem = functools.partial(pltpu.VMEM, dtype=jnp.float32)
    tile = (levels, block)
    in_vmem = pl.BlockSpec(memory_space=pltpu.VMEM)
    in_smem = pl.BlockSpec(memory_space=pltpu.SMEM)
    slots_all = columns * depth * capacity
    dma = pltpu.SemaphoreType.DMA
    field = pl.pallas_call(
        functools.partial(kernel, (along_x, along_y, depth, inner, capacity)),
        out_shape=jax.ShapeDtypeStruct((frows,) + tile, jnp.float32),
        in_specs=[in_smem, in_smem, in_vmem, pl.BlockSpec(memory_space=pl.ANY), in_vmem],
        out_specs=in_vmem,
        scratch_shapes=[
            vmem((slots_all,) + tile),
            vmem((slots_all,) + tile),
            vmem((frows, fanin * block, block)),
            pltpu.VMEM((frows, fanin * block, block), jnp.bfloat16),
            pltpu.VMEM((frows, fanin * block, block), jnp.bfloat16),
            vmem((full,) + tile), vmem((full,) + tile), vmem((full,) + tile), vmem((full,) + tile),
            vmem((full, 1, block)), vmem((full, 1, block)),
            vmem((len(DIRS), frows, block)),
            vmem((frows // PER_TILE,) + tile),
            vmem((len(DIRS), frows // PER_TILE) + tile),
            dma((columns * depth,)), dma((columns * depth,)),
            dma((2, max(1, depth - 1))), dma((2, max(1, depth - 1))),
            dma((len(DIRS),)), dma((len(DIRS),)), dma((len(DIRS),)), dma((len(DIRS),)),
            dma,
        ] + [vmem((srows,) + tile)] * (2 * (depth - 1)),
        compiler_params=pltpu.CompilerParams(
            collective_id=0, has_side_effects=True, vmem_limit_bytes=48 * 2 ** 20),
        cost_estimate=pl.CostEstimate(
            flops=6 * levels * frows * fanin * block * block, bytes_accessed=16 * 2 ** 20, transcendentals=0),
    )(send_rows, pick, source.transpose(1, 0, 2),
      remap_weights.reshape(frows, fanin * block, block), smoothing)
    return field.transpose(1, 0, 2)


def solution(mesh):
    return jax.shard_map(
        shards,
        mesh=mesh,
        in_specs=(P("lev", "gy", "gx"), P(("gx", "gy"), None, None, None), P(), P(), P("gx", "gy")),
        out_specs=P("lev", "gx", "gy"),
        check_vma=False,
    )
```

time: 146 us -> 46.8 us (0.32)
  waiting for transfers between devices: 85.5 us -> 0 us
  Pallas kernels: 0 us -> 40.9 us
  starting transfers between devices: 37.9 us -> 0 us
  local copies, waits for them, and re-layouts: 12.3 us -> 4.72 us
  matrix products: 6.64 us -> 0 us
  other arithmetic: 2.91 us -> 0.74 us
    all_to_all x1 -> x0, waiting for transfers between devices: 45.9 us -> none  [shards(): lax.all_to_all(outgoing, ('gx', 'gy'), split_axis=1, concat_axis=1, tiled...]
    pallas_call x0 -> x1, Pallas kernels: none -> 40.9 us  [shards(): pl.pallas_call(functools.partial(kernel, (along_x, along_y, depth, inner,...]
    ppermute x12 -> x0, waiting for transfers between devices: 39.6 us -> none  [the longest x6 22.1 us: padded_2(): lax.ppermute(lax.slice_in_dim(block, 0, width, axis=dim), axis, backward)]
    ppermute x12 -> x0, starting transfers between devices: 29.6 us -> none  [the longest x6 21.9 us: padded_2(): lax.ppermute(lax.slice_in_dim(block, block.shape[dim] - width, None, axis...]
    all_to_all x1 -> x0, starting transfers between devices: 8.31 us -> none  [shards(): lax.all_to_all(outgoing, ('gx', 'gy'), split_axis=1, concat_axis=1, tiled...]
    dot_general x1 -> x0, matrix products: 6.64 us -> none  [shards(): jnp.einsum('likc,ikcd->lid', picked, remap_weights, precision=lax.Precisi...]
    gather x2 -> x0, local copies, waits for them, and re-layouts: 5.73 us -> none  [the longest x1 4.97 us: shards(): outgoing = jnp.take(source, send_row, axis=1)]
    select_n x1 -> x0, local copies, waits for them, and re-layouts: 2.56 us -> none  [shards(): outgoing = jnp.take(source, send_row, axis=1)]
  transfers between devices with their start and end apart: 13 -> 0, of which waited for: 10 -> 0; matrix products, arithmetic and copies ran while one was open for 1% -> 0% of each run, Pallas kernels for 0% -> 0%
where the time goes in v1:
time: 46.8 us; the launch traced here: 46.5 us
  Pallas kernels  40.9 us (87%)
  local copies, waits for them, and re-layouts  4.72 us (10%)
  other arithmetic  0.74 us (2%)
    pallas_call x1, Pallas kernels, shards(): pl.pallas_call(functools.partial(kernel, (along_x, along_y, depth, inner,...  40.9 us
    unnamed x5, local copies, waits for them, and re-layouts  2.04 us
    reshape x2, local copies, waits for them, and re-layouts, plane(): table = table.reshape(along_x, depth, inner, frows, fanin)  1.58 us

profile of v1, /device:TPU:0, one launch (start us, length us, event | category | flops | bytes accessed | tf_op | source)
XLA Modules:
  0.0 46.5 jit_solution(12557074625961967101)
XLA Ops:
  0.0 0.8 %reshape.54 = s32[2,4,2,32,4]{3,2,1,0,4:T(2,128)S(1)} reshape(s32[512,4]{0,1:T(4,128)} %param.7) | data formatting | bytes 16384 | tf_op jit(solution)/shard_map/reshape | solution.py:344
  0.8 0.8 %reshape.55 = s32[2,4,2,32,4]{3,2,1,0,4:T(2,128)S(1)} reshape(s32[512,4]{0,1:T(4,128)} %param.8) | data formatting | bytes 16384 | tf_op jit(solution)/shard_map/reshape | solution.py:344
  1.6 0.1 copy.18
  1.7 0.1 broadcast_in_dim.20
  1.9 0.1 copy.17
  2.0 0.1 eq.56
  2.1 0.2 convert_reduce_fusion
  2.4 0.1 broadcast_compare_fusion
  2.4 0.4 select_reduce_fusion
  2.8 0.1 reshape.56.send_rows
  2.9 1.1 %copy.20 = f32[16,32,128]{2,0,1:T(8,128)S(1)} copy(f32[16,32,128]{2,1,0:T(8,128)} %param.5) | data formatting | bytes 524288 | tf_op args[0]
  4.0 0.0 copy-start
  4.0 0.7 %copy-done = f32[32,128]{1,0:T(8,128)S(1)} copy-done((f32[32,128]{1,0:T(8,128)S(1)}, f32[32,128]{1,0:T(8,128)}, u32[]{:S(2)}) %copy-start) | copy-done | bytes 16408
  4.7 40.9 %shard_map.55 = f32[32,16,128]{2,1,0:T(8,128)S(1)} custom-call(s32[256]{0:T(256)S(1)} %reshape.56.send_rows, s32[128]{0:T(128)S(1)} %fusion.2.pick, f32[32,16,128]{2,1,0:T(8,128)S(1)} %bitcast.26, f32[32,512,128]{2,1,0:T(8,128)} %bitcast.27, f32[32,128]{1,0:T(8,128)S(1)} %copy-done), custom_call_target="tpu_custom_call" | custom-call | flops 201326592 | bytes 16777216 | tf_op jit(solution)/shard_map/pallas_call | solution.py:369
  45.7 0.8 %copy.16 = f32[16,32,128]{2,1,0:T(8,128)} copy(f32[16,32,128]{2,0,1:T(8,128)S(1)} %bitcast.25) | data formatting | bytes 524288 | tf_op jit(solution)/shard_map/transpose | solution.py:396
  (5 shorter events, 0.1 us)
Async XLA Ops:
  4.0 0.7 %copy-start = (f32[32,128]{1,0:T(8,128)S(1)}, f32[32,128]{1,0:T(8,128)}, u32[]{:S(2)}) copy-start(f32[32,128]{1,0:T(8,128)} %smooth.1) | copy-start | bytes 49156

commit v2 on v1

v2 whole, which is shorter than its diff:
```python
import functools

import jax
import jax.numpy as jnp
from jax import lax
from jax.experimental import pallas as pl
from jax.experimental.pallas import tpu as pltpu
from jax.sharding import PartitionSpec as P

PASSES = 3
MESH = pl.DeviceIdType.MESH
DIRS = [(dx, dy) for dx in (-1, 0, 1) for dy in (-1, 0, 1) if (dx, dy) != (0, 0)]
OPPOSITE = [DIRS.index((-dx, -dy)) for dx, dy in DIRS]
LANES = 128
STRIP = 8
PER_TILE = LANES // STRIP
HALVES = 2
W_PIECES = 4
GROUP = 4


def layout(along_x, along_y, capacity, rows):
    inner = 2 if along_y % 2 == 0 else 1
    if capacity * inner * along_x > rows:
        return along_y // inner, inner
    return 1, along_y


def kernel(dims, send_rows, pick, src, weights, smooth, out, inbox_0, inbox_1, outbox, w_full, w_high, w_low,
           main_a, main_b, side_a, side_b, s_main, s_side, s_in, edge, edge_in,
           send_sem, recv_sem, chain_send, chain_recv, s_send, s_recv, h_send, h_recv, w_sem, *chunks):
    along_x, along_y, depth, inner, capacity = dims
    frows, fan = w_full.shape[0], pick.shape[0] // w_full.shape[0]
    levels, srows = src.shape[:2]
    sub = levels // HALVES
    width = LANES // HALVES
    columns = along_x * inner
    inboxes = (inbox_0, inbox_1)
    own, chain = chunks[:HALVES], chunks[HALVES:]
    ups = [chain[h * (depth - 1):(h + 1) * (depth - 1)] for h in range(HALVES)]
    downs = [chain[(HALVES + h) * (depth - 1):(HALVES + h + 1) * (depth - 1)] for h in range(HALVES)]
    x, y, lev = lax.axis_index("gx"), lax.axis_index("gy"), lax.axis_index("lev")
    z, yi = y // inner, y % inner
    column = x * inner + yi
    lane = lax.broadcasted_iota(jnp.int32, (levels, LANES), 1)
    lane_8 = lax.broadcasted_iota(jnp.int32, (sub, LANES), 1)
    tiles = frows // PER_TILE
    at = {d: k for k, d in enumerate(DIRS)}

    def column_id(c):
        return (c // inner, z * inner + c % inner, lev)

    def near(dx, dy):
        ok = jnp.logical_and(
            jnp.logical_and(x + dx >= 0, x + dx < along_x),
            jnp.logical_and(y + dy >= 0, y + dy < along_y),
        )
        return ok, (x + dx, y + dy, lev)

    barrier = pltpu.get_barrier_semaphore()

    def greet(device):
        pl.semaphore_signal(barrier, inc=1, device_id=device, device_id_type=MESH)

    def greet_column(q, carry):
        greet(column_id(lax.rem(column + q, columns)))
        return carry

    lax.fori_loop(1, columns, greet_column, 0)
    total = columns - 1
    links = [near(dx, dy) for dx, dy in DIRS]
    if depth > 1:
        links = links + [(z < depth - 1, (x, y + inner, lev)), (z > 0, (x, y - inner, lev))]
    for ok, device in links:
        total = total + ok.astype(jnp.int32)

        @pl.when(ok)
        def _():
            greet(device)

    share = frows // W_PIECES

    def w_copy(n):
        rows = pl.ds(n * share, share)
        return pltpu.make_async_copy(weights.at[rows], w_full.at[rows], w_sem.at[n])

    for n in range(W_PIECES):
        w_copy(n).start()

    def swapped(value):
        return pltpu.roll(value, width, axis=1)

    for b in range(srows // 8):
        for l in range(sub):
            low, high = src[l, 8 * b:8 * b + 8, :], src[sub + l, 8 * b:8 * b + 8, :]
            place = pl.ds(8 * b, 8)
            own[0][place, l, :] = jnp.where(lane_8 < width, low, swapped(high))
            own[1][place, l, :] = jnp.where(lane_8 < width, swapped(low), high)

    pl.semaphore_wait(barrier, total)

    def chain_copy(h, up, t):
        boxes = (ups if up else downs)[h]
        return pltpu.make_async_remote_copy(
            src_ref=own[h] if t == 0 else boxes[t - 1], dst_ref=boxes[t],
            send_sem=chain_send.at[h, 0 if up else 1, t], recv_sem=chain_recv.at[h, 0 if up else 1, t],
            device_id=(x, y + (inner if up else -inner), lev), device_id_type=MESH)

    def slot_copy(h, q, tile):
        c = lax.rem(column + q, columns)
        sem = (h * columns + q) * depth + tile
        return pltpu.make_async_remote_copy(
            src_ref=outbox.at[h, pl.ds((c * depth + tile) * capacity, capacity)],
            dst_ref=inboxes[h].at[pl.ds((column * depth + tile) * capacity, capacity)],
            send_sem=send_sem.at[sem], recv_sem=recv_sem.at[sem],
            device_id=column_id(c), device_id_type=MESH)

    def ship(h, chunk, tile):
        def block(n):
            return chunk[send_rows[n]]

        def peer(q, carry):
            base = (lax.rem(column + q, columns) * depth + tile) * capacity
            for j in range(capacity):
                outbox[h, base + j] = block(base + j)
            slot_copy(h, q, tile).start()
            return carry

        lax.fori_loop(1, columns, peer, 0)
        base = (column * depth + tile) * capacity
        for j in range(capacity):
            inboxes[h][base + j] = block(base + j)

    def start_chain(h):
        if depth > 1:
            @pl.when(z < depth - 1)
            def _():
                chain_copy(h, True, 0).start()

            @pl.when(z > 0)
            def _():
                chain_copy(h, False, 0).start()

    def pass_on(h, t):
        for up, ok, onward in ((True, z >= t + 1, z < depth - 1), (False, z + 1 + t <= depth - 1, z > 0)):
            @pl.when(ok)
            def _():
                chain_copy(h, up, t).wait_recv()
                if t + 1 < depth - 1:
                    @pl.when(onward)
                    def _():
                        chain_copy(h, up, t + 1).start()
                ship(h, (ups if up else downs)[h][t], z - 1 - t if up else z + 1 + t)

    def s_copy(k):
        ok, device = near(*DIRS[k])
        return ok, pltpu.make_async_remote_copy(
            src_ref=smooth, dst_ref=s_in.at[OPPOSITE[k]], send_sem=s_send.at[k],
            recv_sem=s_recv.at[OPPOSITE[k]], device_id=device, device_id_type=MESH)

    def h_copy(k, tile):
        dx, dy = DIRS[k]
        ok, device = near(dx, dy)
        if dy == 0:
            source = main_a.at[pl.ds(frows if dx > 0 else PASSES, PASSES)]
            target = main_a.at[pl.ds(0 if dx > 0 else frows + PASSES, PASSES)]
        else:
            source, target = edge.at[tile], edge_in.at[OPPOSITE[k], tile]
        return ok, pltpu.make_async_remote_copy(
            src_ref=source, dst_ref=target, send_sem=h_send.at[k, tile],
            recv_sem=h_recv.at[OPPOSITE[k], tile], device_id=device, device_id_type=MESH)

    def split_weights(n):
        w_copy(n).wait()

        def one(i, carry):
            for k in range(fan):
                for h in range(HALVES):
                    value = w_full[i, pl.ds(k * LANES + h * width, width), :]
                    high = value.astype(jnp.bfloat16)
                    place = pl.ds(k * width, width)
                    w_high[h, i, place, :] = high
                    w_low[h, i, place, :] = (value - high.astype(jnp.float32)).astype(jnp.bfloat16)
            return carry

        lax.fori_loop(n * share, (n + 1) * share, one, 0)

    def product(h, i):
        rows = [[], []]
        for k in range(0, fan, 2):
            even, odd = inboxes[h][pick[i * fan + k]], inboxes[h][pick[i * fan + k + 1]]
            rows[0].append(jnp.where(lane_8 < width, even, swapped(odd)))
            rows[1].append(jnp.where(lane_8 < width, swapped(even), odd))
        blocks = jnp.concatenate([jnp.concatenate(r, axis=1) for r in rows], axis=0)
        high = blocks.astype(jnp.bfloat16)
        low = (blocks - high.astype(jnp.float32)).astype(jnp.bfloat16)
        both = jnp.dot(jnp.concatenate([high, low], axis=0), w_high[h, i], preferred_element_type=jnp.float32)
        rest = jnp.dot(high, w_low[h, i], preferred_element_type=jnp.float32)
        result = both[:levels] + (both[levels:] + rest)
        if h == 0:
            main_a[PASSES + i] = result
        else:
            main_a[PASSES + i] += result

    groups = frows // GROUP

    def products(h, start, stop):
        def some(n, carry):
            for j in range(GROUP):
                product(h, n * GROUP + j)
            return carry

        lax.fori_loop(start, stop, some, 0)

    def landed(h):
        def one(n, carry):
            slot_copy(h, n // depth, lax.rem(n, depth)).wait_recv()
            return carry

        lax.fori_loop(depth, columns * depth, one, 0)

    start_chain(0)
    ship(0, own[0], z)
    for k in range(len(DIRS)):
        ok, copy = s_copy(k)

        @pl.when(ok)
        def _():
            copy.start()

    for k, (dx, dy) in enumerate(DIRS):
        ok, _ = near(dx, dy)

        @pl.when(jnp.logical_not(ok))
        def _():
            s_in[k] = jnp.zeros(s_in.shape[1:], jnp.float32)
            if dy == 0:
                main_a[pl.ds(0 if dx < 0 else frows + PASSES, PASSES)] = jnp.zeros(
                    (PASSES,) + main_a.shape[1:], jnp.float32)
            else:
                edge_in[k] = jnp.zeros(edge_in.shape[1:], jnp.float32)

    second = min(1, depth - 2)
    done = 0
    for t in range(depth - 1):
        pass_on(0, t)
        if t == second:
            start_chain(1)
        if done < W_PIECES:
            split_weights(done)
            done += 1

    ship(1, own[1], z)
    for n in range(done, W_PIECES):
        split_weights(n)

    for k in range(len(DIRS)):
        ok, copy = s_copy(k)

        @pl.when(ok)
        def _():
            copy.wait_send()
            arrival_wait(s_in.at[k], smooth, s_recv.at[k])

    row_lane = lax.broadcasted_iota(jnp.int32, (1, LANES), 1)

    def side(left, right):
        return jnp.where(row_lane < PASSES, right, jnp.where(row_lane >= LANES - PASSES, left, 0.0))

    for i in range(frows):
        s_main[PASSES + i] = smooth[i:i + 1, :]
        s_side[PASSES + i] = side(s_in[at[0, -1], i:i + 1, :], s_in[at[0, 1], i:i + 1, :])
    for i in range(PASSES):
        low, high = frows - PASSES + i, frows + PASSES + i
        s_main[i] = s_in[at[-1, 0], low:low + 1, :]
        s_side[i] = side(s_in[at[-1, -1], low:low + 1, :], s_in[at[-1, 1], low:low + 1, :])
        s_main[high] = s_in[at[1, 0], i:i + 1, :]
        s_side[high] = side(s_in[at[1, -1], i:i + 1, :], s_in[at[1, 1], i:i + 1, :])

    steps = max(1, depth - 1)
    for t in range(steps):
        if t < depth - 1:
            pass_on(1, t)
        if t == 0:
            landed(0)
        products(0, groups * t // steps, groups * (t + 1) // steps)
    landed(1)

    def send_halo(wanted):
        for k, (dx, dy) in enumerate(DIRS):
            for tile in wanted(dx, dy):
                ok, copy = h_copy(k, tile)

                @pl.when(ok)
                def _():
                    copy.start()

    def halo_tiles(dx, dy):
        if dy == 0:
            return [0]
        return list(range(tiles)) if dx == 0 else [0 if dx < 0 else tiles - 1]

    def pack(b):
        packed = jnp.zeros((levels, LANES), jnp.float32)
        for j in range(PER_TILE):
            moved = pltpu.roll(main_a[PASSES + b * PER_TILE + j], STRIP * j + STRIP // 2, axis=1)
            packed = jnp.where(lane // STRIP == j, moved, packed)
        edge[b] = packed
        send_halo(lambda dx, dy: [b] if dy != 0 and b in halo_tiles(dx, dy) else [])

    products(1, 0, 1)
    products(1, groups - 1, groups)
    send_halo(lambda dx, dy: [0] if dy == 0 else [])
    for b in range(tiles):
        products(1, max(1, b * groups // tiles), min(groups - 1, (b + 1) * groups // tiles))
        pack(b)

    def sent(n, carry):
        for h in range(HALVES):
            slot_copy(h, n // depth, lax.rem(n, depth)).wait_send()
        return carry

    lax.fori_loop(depth, columns * depth, sent, 0)
    for t in range(depth - 1):
        for h in range(HALVES):
            @pl.when(jnp.logical_and(z < depth - 1, z - t >= 0))
            def _():
                chain_copy(h, True, t).wait_send()

            @pl.when(jnp.logical_and(z > 0, z + t <= depth - 1))
            def _():
                chain_copy(h, False, t).wait_send()

    for k, (dx, dy) in enumerate(DIRS):
        for tile in halo_tiles(dx, dy):
            ok, copy = h_copy(k, tile)

            @pl.when(ok)
            def _():
                copy.wait_send()

        for tile in halo_tiles(-dx, -dy):
            @pl.when(near(dx, dy)[0])
            def _():
                if dy == 0:
                    rows = main_a.at[pl.ds(0 if dx < 0 else frows + PASSES, PASSES)]
                    arrival_wait(rows, rows, h_recv.at[k, tile])
                else:
                    arrival_wait(edge_in.at[k, tile], edge.at[tile], h_recv.at[k, tile])

    inside = jnp.logical_or(lane < PASSES, lane >= LANES - PASSES)

    def unpack(row, tile, place, left, right):
        merged = jnp.where(lax.rem(lane, STRIP) < STRIP // 2, edge_in[left, tile], edge_in[right, tile])
        moved = pltpu.roll(merged, (2 * LANES - STRIP * place - STRIP // 2) % LANES, axis=1)
        side_a[row] = jnp.where(inside, moved, 0.0)

    for i in range(frows):
        unpack(PASSES + i, i // PER_TILE, i % PER_TILE, at[0, -1], at[0, 1])
    for i in range(PASSES):
        far = frows - PASSES + i
        unpack(i, far // PER_TILE, far % PER_TILE, at[-1, -1], at[-1, 1])
        unpack(frows + PASSES + i, 0, i, at[1, -1], at[1, 1])

    first, last = lane == 0, lane == LANES - 1

    def smooth_row(r, main, sides, write):
        u, h = main[r], sides[r]
        u_up, u_down = pltpu.roll(u, 1, axis=1), pltpu.roll(u, LANES - 1, axis=1)
        h_up, h_down = pltpu.roll(h, 1, axis=1), pltpu.roll(h, LANES - 1, axis=1)
        lap = (main[r + 1] + main[r - 1] + jnp.where(last, h_down, u_down)
               + jnp.where(first, h_up, u_up) - 4.0 * u)
        lap_h = (sides[r + 1] + sides[r - 1] + jnp.where(last, u_down, h_down)
                 + jnp.where(first, u_up, h_up) - 4.0 * h)
        write(r, u + s_main[r] * lap, h + s_side[r] * lap_h)

    def write_b(r, u, h):
        main_b[r] = u
        side_b[r] = h

    def write_a(r, u, h):
        main_a[r] = u
        side_a[r] = h

    def write_out(r, u, h):
        out[pl.ds(r - PASSES, levels, stride=frows), :] = u

    for p, (main, sides, write) in enumerate((
            (main_a, side_a, write_b), (main_b, side_b, write_a), (main_a, side_a, write_out))):
        start, count = p + 1, frows + 2 * PASSES - 2 * (p + 1)
        chunk = 4 if count % 4 == 0 else 2

        def rows(n, carry):
            for j in range(chunk):
                smooth_row(start + n * chunk + j, main, sides, write)
            return carry

        lax.fori_loop(0, count // chunk, rows, 0)


def arrival_wait(target, source, sem):
    pltpu.make_async_copy(source, target, sem).wait()


def shards(source, remap_weights, intersection_devices, intersection_rows, smoothing):
    along_x = lax.axis_size("gx")
    along_y = lax.axis_size("gy")
    devices = along_x * along_y
    frows, fanin, block = remap_weights.shape[:3]
    levels, srows = source.shape[:2]
    capacity = 2 * max(1, frows * fanin // devices)
    depth, inner = layout(along_x, along_y, capacity, srows)
    columns = along_x * inner
    x, y = lax.axis_index("gx"), lax.axis_index("gy")
    z, yi = y // inner, y % inner
    column = x * inner + yi

    codes = intersection_devices * srows + intersection_rows
    plane = jnp.concatenate([
        lax.dynamic_slice_in_dim(codes, (i * along_y + z * inner) * frows, inner * frows, 0) for i in range(along_x)])
    plane = plane.reshape(columns, frows * fanin)
    entries, lats = plane // srows, plane % srows
    order = jnp.arange(frows * fanin)
    same = jnp.logical_and(entries[:, :, None] == entries[:, None, :], order[None, :] < order[:, None])
    slots = jnp.sum(same.astype(jnp.int32), axis=2)
    tiles = x * along_y + jnp.arange(depth) * inner + yi
    matched = jnp.logical_and(
        entries[:, None, None, :] == tiles[None, :, None, None],
        slots[:, None, None, :] == jnp.arange(capacity)[None, None, :, None])
    send_rows = jnp.sum(jnp.where(matched, lats[:, None, None, :], 0), axis=3).reshape(-1)
    mine = lax.dynamic_index_in_dim(entries, column, 0, keepdims=False)
    my_slots = lax.dynamic_index_in_dim(slots, column, 0, keepdims=False)
    my_y = mine % along_y
    pick = (((mine // along_y) * inner + my_y % inner) * depth + my_y // inner) * capacity + my_slots

    full = frows + 2 * PASSES
    sub = levels // HALVES
    vmem = functools.partial(pltpu.VMEM, dtype=jnp.float32)
    tile = (levels, block)
    in_vmem = pl.BlockSpec(memory_space=pltpu.VMEM)
    in_smem = pl.BlockSpec(memory_space=pltpu.SMEM)
    slots_all = columns * depth * capacity
    dma = pltpu.SemaphoreType.DMA
    sides = len(DIRS)
    edges = frows // PER_TILE
    halves = pltpu.VMEM((HALVES, frows, fanin * block // HALVES, block), jnp.bfloat16)
    field = pl.pallas_call(
        functools.partial(kernel, (along_x, along_y, depth, inner, capacity)),
        out_shape=jax.ShapeDtypeStruct((levels * frows, block), jnp.float32),
        in_specs=[in_smem, in_smem, in_vmem, pl.BlockSpec(memory_space=pl.ANY), in_vmem],
        out_specs=in_vmem,
        scratch_shapes=[
            vmem((slots_all, sub, block)), vmem((slots_all, sub, block)),
            vmem((HALVES, slots_all, sub, block)),
            vmem((frows, fanin * block, block)),
            halves, halves,
            vmem((full,) + tile), vmem((full,) + tile), vmem((full,) + tile), vmem((full,) + tile),
            vmem((full, 1, block)), vmem((full, 1, block)),
            vmem((sides, frows, block)),
            vmem((edges,) + tile),
            vmem((sides, edges) + tile),
            dma((HALVES * columns * depth,)), dma((HALVES * columns * depth,)),
            dma((HALVES, 2, max(1, depth - 1))), dma((HALVES, 2, max(1, depth - 1))),
            dma((sides,)), dma((sides,)), dma((sides, edges)), dma((sides, edges)),
            dma((W_PIECES,)),
        ] + [vmem((srows, sub, block))] * (HALVES + 2 * HALVES * (depth - 1)),
        compiler_params=pltpu.CompilerParams(
            collective_id=0, has_side_effects=True, vmem_limit_bytes=48 * 2 ** 20),
        cost_estimate=pl.CostEstimate(
            flops=6 * levels * frows * fanin * block * block, bytes_accessed=16 * 2 ** 20, transcendentals=0),
    )(send_rows, pick, source, remap_weights.reshape(frows, fanin * block, block), smoothing)
    return field.reshape(levels, frows, block)


def solution(mesh):
    return jax.shard_map(
        shards,
        mesh=mesh,
        in_specs=(P("lev", "gy", "gx"), P(("gx", "gy"), None, None, None), P(), P(), P("gx", "gy")),
        out_specs=P("lev", "gx", "gy"),
        check_vma=False,
    )
```

time: 46.8 us -> 47 us (level)
  local copies, waits for them, and re-layouts: 4.72 us -> 2.76 us
  Pallas kernels: 40.9 us -> 42.3 us
  other arithmetic: 0.74 us -> 1.55 us
    reshape x2 -> x1, local copies, waits for them, and re-layouts: 1.58 us -> 0.11 us  [shards(): plane = plane.reshape(columns, frows * fanin)]
    pallas_call x1, Pallas kernels: 40.9 us -> 42.3 us  [shards(): pl.pallas_call(functools.partial(kernel, (along_x, along_y, depth, inner,...]
    transpose x1 -> x0, local copies, waits for them, and re-layouts: 0.78 us -> none  [shards(): return field.transpose(1, 0, 2)]
    add x0 -> x1, other arithmetic: none -> 0.72 us  [shards(): codes = intersection_devices * srows + intersection_rows]
where the time goes in v2:
time: 47 us; the launch traced here: 46.7 us
  Pallas kernels  42.3 us (90%)
  local copies, waits for them, and re-layouts  2.76 us (6%)
  other arithmetic  1.55 us (3%)
    pallas_call x1, Pallas kernels, shards(): pl.pallas_call(functools.partial(kernel, (along_x, along_y, depth, inner,...  42.3 us
    unnamed x5, local copies, waits for them, and re-layouts  2.38 us

profile of v2, /device:TPU:0, one launch (start us, length us, event | category | flops | bytes accessed | tf_op | source)
XLA Modules:
  0.0 46.7 jit_solution(2087172210079370895)
XLA Ops:
  0.0 0.7 %multiply_add_fusion = s32[512,4]{0,1:T(4,128)S(1)} fusion(s32[512,4]{0,1:T(4,128)} %param.8, s32[512,4]{0,1:T(4,128)} %param.7), kind=kLoop, calls=%fused_computation.4 | loop fusion | flops 4096 | bytes 24576 | tf_op jit(solution)/shard_map/add | solution.py:418
  0.7 0.1 constant_dynamic-slice_fusion.3
  0.8 0.1 pad_add_fusion
  0.9 0.1 copy.7
  1.0 0.1 reshape.149
  1.1 0.2 convert_reduce_fusion
  1.4 0.1 broadcast_compare_fusion
  1.5 0.4 select_reduce_fusion
  1.9 0.1 reshape.150.send_rows
  2.0 0.0 copy-start
  2.0 1.0 %copy-done = f32[16,32,128]{2,1,0:T(8,128)S(1)} copy-done((f32[16,32,128]{2,1,0:T(8,128)S(1)}, f32[16,32,128]{2,1,0:T(8,128)}, u32[]{:S(2)}) %copy-start) | copy-done | bytes 262168
  2.9 0.0 copy-start.1
  2.9 0.7 %copy-done.1 = f32[32,128]{1,0:T(8,128)S(1)} copy-done((f32[32,128]{1,0:T(8,128)S(1)}, f32[32,128]{1,0:T(8,128)}, u32[]{:S(2)}) %copy-start.1) | copy-done | bytes 16408
  3.6 42.3 %shard_map.55 = f32[512,128]{1,0:T(8,128)S(1)} custom-call(s32[256]{0:T(256)S(1)} %reshape.150.send_rows, s32[128]{0:T(128)S(1)} %fusion.4.pick, f32[16,32,128]{2,1,0:T(8,128)S(1)} %copy-done, f32[32,512,128]{2,1,0:T(8,128)} %bitcast.11, f32[32,128]{1,0:T(8,128)S(1)} %copy-done.1), custom_call_target="tpu_custom_call" | custom-call | flops 201326592 | bytes 16777216 | tf_op jit(solution)/shard_map/pallas_call | solution.py:447
  46.0 0.7 %copy.9 = f32[16,32,128]{2,1,0:T(8,128)} copy(f32[16,32,128]{2,1,0:T(8,128)S(1)} %bitcast.10) | data formatting | bytes 524288
  (5 shorter events, 0.1 us)
Async XLA Ops:
  2.0 1.0 %copy-start = (f32[16,32,128]{2,1,0:T(8,128)S(1)}, f32[16,32,128]{2,1,0:T(8,128)}, u32[]{:S(2)}) copy-start(f32[16,32,128]{2,1,0:T(8,128)} %src.1) | copy-start | bytes 786436
  2.9 0.7 %copy-start.1 = (f32[32,128]{1,0:T(8,128)S(1)}, f32[32,128]{1,0:T(8,128)}, u32[]{:S(2)}) copy-start(f32[32,128]{1,0:T(8,128)} %smooth.1) | copy-start | bytes 49156

commit v3 on v2

--- a/solution.py
+++ b/solution.py
@@ -16,7 +16,7 @@
 PER_TILE = LANES // STRIP
 HALVES = 2
 W_PIECES = 4
-GROUP = 4
+GROUP = 8
 
 
 def layout(along_x, along_y, capacity, rows):
@@ -26,11 +26,12 @@
     return 1, along_y
 
 
-def kernel(dims, send_rows, pick, src, weights, smooth, out, inbox_0, inbox_1, outbox, w_full, w_high, w_low,
+def kernel(dims, devices_in, rows_in, src_in, weights, smooth_in, out, devices, lat, src, smooth,
+           table_v, pick_v, table, pick, inbox_0, inbox_1, outbox, w_full, w_high, w_low,
            main_a, main_b, side_a, side_b, s_main, s_side, s_in, edge, edge_in,
-           send_sem, recv_sem, chain_send, chain_recv, s_send, s_recv, h_send, h_recv, w_sem, *chunks):
+           send_sem, recv_sem, chain_send, chain_recv, s_send, s_recv, h_send, h_recv, w_sem, in_sem, *chunks):
     along_x, along_y, depth, inner, capacity = dims
-    frows, fan = w_full.shape[0], pick.shape[0] // w_full.shape[0]
+    frows, fan = w_full.shape[0], devices.shape[0]
     levels, srows = src.shape[:2]
     sub = levels // HALVES
     width = LANES // HALVES
@@ -57,6 +58,11 @@
         )
         return ok, (x + dx, y + dy, lev)
 
+    loads = [pltpu.make_async_copy(a, b, in_sem.at[n]) for n, (a, b) in enumerate((
+        (src_in, src), (devices_in, devices), (rows_in, lat), (smooth_in, smooth)))]
+    for load in loads:
+        load.start()
+
     barrier = pltpu.get_barrier_semaphore()
 
     def greet(device):
@@ -87,6 +93,65 @@
     for n in range(W_PIECES):
         w_copy(n).start()
 
+    for load in loads[1:]:
+        load.wait()
+    me = x * along_y + y
+    wide = (LANES, LANES)
+    from_lane = lax.broadcasted_iota(jnp.int32, wide, 0)
+    to_lane = lax.broadcasted_iota(jnp.int32, wide, 1)
+    together = from_lane // frows == to_lane // frows
+    group_ones = jnp.where(together, 1.0, 0.0).astype(jnp.bfloat16)
+    earlier = jnp.where(jnp.logical_and(together, from_lane < to_lane), 1.0, 0.0).astype(jnp.bfloat16)
+
+    def count(hits, matrix):
+        return jnp.dot(hits.astype(jnp.bfloat16), matrix, preferred_element_type=jnp.float32)
+
+    def ranks(hits):
+        found, before = [], None
+        for k in range(fan):
+            within = count(hits[k], earlier)
+            found.append(within if before is None else within + before)
+            if k + 1 < fan:
+                whole = count(hits[k], group_ones)
+                before = whole if before is None else before + whole
+        return found
+
+    groups_in_tile = LANES // frows
+    slot = lax.broadcasted_iota(jnp.int32, (capacity, LANES), 0).astype(jnp.float32)
+    mine = lax.broadcasted_iota(jnp.int32, (max(8, depth), LANES), 0) * inner + x * along_y + yi
+    rows_of = jnp.zeros((depth * capacity, LANES), jnp.float32)
+    for n in range(devices.shape[1] // LANES):
+        span = slice(n * LANES, (n + 1) * LANES)
+        hits = [jnp.where(devices[k:k + 1, span] == mine, 1.0, 0.0) for k in range(fan)]
+        found = ranks(hits)
+        parts = []
+        for t in range(depth):
+            part = jnp.zeros((capacity, LANES), jnp.float32)
+            for k in range(fan):
+                rank = jnp.where(hits[k][t:t + 1] > 0.5, found[k][t:t + 1], -1.0)
+                part = part + jnp.where(rank == slot, lat[k:k + 1, span].astype(jnp.float32), 0.0)
+            parts.append(part)
+        gather = jnp.where(from_lane // frows + n * groups_in_tile == to_lane, 1.0, 0.0).astype(jnp.bfloat16)
+        rows_of = rows_of + count(jnp.concatenate(parts, axis=0) if depth > 1 else parts[0], gather)
+    table_v[...] = jnp.clip(rows_of.astype(jnp.int32), 0, srows - 1)
+
+    span = pl.ds(pl.multiple_of(me // groups_in_tile * LANES, LANES), LANES)
+    every = lax.broadcasted_iota(jnp.int32, (along_x * along_y, LANES), 0)
+    named = [devices[k:k + 1, span] for k in range(fan)]
+    hits = [jnp.where(named[k] == every, 1.0, 0.0) for k in range(fan)]
+    found = ranks(hits)
+    for k in range(fan):
+        rank = jnp.sum(hits[k] * found[k], axis=0, keepdims=True).astype(jnp.int32)
+        tile_y = lax.rem(named[k], along_y)
+        base = (named[k] // along_y * inner + lax.rem(tile_y, inner)) * depth + tile_y // inner
+        pick_v[k:k + 1, :] = jnp.clip(base * capacity + rank, 0, columns * depth * capacity - 1)
+    tables = [pltpu.make_async_copy(a, b, in_sem.at[4 + n]) for n, (a, b) in enumerate((
+        (table_v, table), (pick_v, pick)))]
+    for copy in tables:
+        copy.start()
+    my_lane = lax.rem(me, groups_in_tile) * frows
+    loads[0].wait()
+
     def swapped(value):
         return pltpu.roll(value, width, axis=1)
 
@@ -97,6 +162,8 @@
             own[0][place, l, :] = jnp.where(lane_8 < width, low, swapped(high))
             own[1][place, l, :] = jnp.where(lane_8 < width, swapped(low), high)
 
+    for copy in tables:
+        copy.wait()
     pl.semaphore_wait(barrier, total)
 
     def chain_copy(h, up, t):
@@ -116,20 +183,24 @@
             device_id=column_id(c), device_id_type=MESH)
 
     def ship(h, chunk, tile):
-        def block(n):
-            return chunk[send_rows[n]]
+        def fill(c, write):
+            owner = c // inner * along_y + z * inner + lax.rem(c, inner)
+            for j in range(capacity):
+                write((c * depth + tile) * capacity + j, chunk[table[tile * capacity + j, owner]])
+
+        def to_outbox(n, value):
+            outbox[h, n] = value
+
+        def to_inbox(n, value):
+            inboxes[h][n] = value
 
         def peer(q, carry):
-            base = (lax.rem(column + q, columns) * depth + tile) * capacity
-            for j in range(capacity):
-                outbox[h, base + j] = block(base + j)
+            fill(lax.rem(column + q, columns), to_outbox)
             slot_copy(h, q, tile).start()
             return carry
 
         lax.fori_loop(1, columns, peer, 0)
-        base = (column * depth + tile) * capacity
-        for j in range(capacity):
-            inboxes[h][base + j] = block(base + j)
+        fill(column, to_inbox)
 
     def start_chain(h):
         if depth > 1:
@@ -188,7 +259,7 @@
     def product(h, i):
         rows = [[], []]
         for k in range(0, fan, 2):
-            even, odd = inboxes[h][pick[i * fan + k]], inboxes[h][pick[i * fan + k + 1]]
+            even, odd = (inboxes[h][pick[k + j, my_lane + i]] for j in range(2))
             rows[0].append(jnp.where(lane_8 < width, even, swapped(odd)))
             rows[1].append(jnp.where(lane_8 < width, swapped(even), odd))
         blocks = jnp.concatenate([jnp.concatenate(r, axis=1) for r in rows], axis=0)
@@ -221,6 +292,7 @@
 
     start_chain(0)
     ship(0, own[0], z)
+    ship(1, own[1], z)
     for k in range(len(DIRS)):
         ok, copy = s_copy(k)
 
@@ -240,17 +312,15 @@
             else:
                 edge_in[k] = jnp.zeros(edge_in.shape[1:], jnp.float32)
 
-    second = min(1, depth - 2)
     done = 0
-    for t in range(depth - 1):
-        pass_on(0, t)
-        if t == second:
+    events = sorted((t + 1.5 * h, h, t) for h in range(HALVES) for t in range(depth - 1))
+    for n, (_, h, t) in enumerate(events):
+        pass_on(h, t)
+        if n == 0:
             start_chain(1)
         if done < W_PIECES:
             split_weights(done)
             done += 1
-
-    ship(1, own[1], z)
     for n in range(done, W_PIECES):
         split_weights(n)
 
@@ -277,13 +347,8 @@
         s_main[high] = s_in[at[1, 0], i:i + 1, :]
         s_side[high] = side(s_in[at[1, -1], i:i + 1, :], s_in[at[1, 1], i:i + 1, :])
 
-    steps = max(1, depth - 1)
-    for t in range(steps):
-        if t < depth - 1:
-            pass_on(1, t)
-        if t == 0:
-            landed(0)
-        products(0, groups * t // steps, groups * (t + 1) // steps)
+    landed(0)
+    products(0, 0, groups)
     landed(1)
 
     def send_halo(wanted):
@@ -388,7 +453,7 @@
     for p, (main, sides, write) in enumerate((
             (main_a, side_a, write_b), (main_b, side_b, write_a), (main_a, side_a, write_out))):
         start, count = p + 1, frows + 2 * PASSES - 2 * (p + 1)
-        chunk = 4 if count % 4 == 0 else 2
+        chunk = next(n for n in (12, 17, 16, 2, 1) if count % n == 0)
 
         def rows(n, carry):
             for j in range(chunk):
@@ -411,34 +476,14 @@
     capacity = 2 * max(1, frows * fanin // devices)
     depth, inner = layout(along_x, along_y, capacity, srows)
     columns = along_x * inner
-    x, y = lax.axis_index("gx"), lax.axis_index("gy")
-    z, yi = y // inner, y % inner
-    column = x * inner + yi
-
-    codes = intersection_devices * srows + intersection_rows
-    plane = jnp.concatenate([
-        lax.dynamic_slice_in_dim(codes, (i * along_y + z * inner) * frows, inner * frows, 0) for i in range(along_x)])
-    plane = plane.reshape(columns, frows * fanin)
-    entries, lats = plane // srows, plane % srows
-    order = jnp.arange(frows * fanin)
-    same = jnp.logical_and(entries[:, :, None] == entries[:, None, :], order[None, :] < order[:, None])
-    slots = jnp.sum(same.astype(jnp.int32), axis=2)
-    tiles = x * along_y + jnp.arange(depth) * inner + yi
-    matched = jnp.logical_and(
-        entries[:, None, None, :] == tiles[None, :, None, None],
-        slots[:, None, None, :] == jnp.arange(capacity)[None, None, :, None])
-    send_rows = jnp.sum(jnp.where(matched, lats[:, None, None, :], 0), axis=3).reshape(-1)
-    mine = lax.dynamic_index_in_dim(entries, column, 0, keepdims=False)
-    my_slots = lax.dynamic_index_in_dim(slots, column, 0, keepdims=False)
-    my_y = mine % along_y
-    pick = (((mine // along_y) * inner + my_y % inner) * depth + my_y // inner) * capacity + my_slots
-
     full = frows + 2 * PASSES
     sub = levels // HALVES
     vmem = functools.partial(pltpu.VMEM, dtype=jnp.float32)
     tile = (levels, block)
     in_vmem = pl.BlockSpec(memory_space=pltpu.VMEM)
-    in_smem = pl.BlockSpec(memory_space=pltpu.SMEM)
+    anywhere = pl.BlockSpec(memory_space=pl.ANY)
+    entries = (fanin, intersection_devices.shape[0])
+    tables = ((depth * capacity, block), (fanin, block))
     slots_all = columns * depth * capacity
     dma = pltpu.SemaphoreType.DMA
     sides = len(DIRS)
@@ -447,9 +492,13 @@
     field = pl.pallas_call(
         functools.partial(kernel, (along_x, along_y, depth, inner, capacity)),
         out_shape=jax.ShapeDtypeStruct((levels * frows, block), jnp.float32),
-        in_specs=[in_smem, in_smem, in_vmem, pl.BlockSpec(memory_space=pl.ANY), in_vmem],
+        in_specs=[anywhere] * 5,
         out_specs=in_vmem,
         scratch_shapes=[
+            pltpu.VMEM(entries, jnp.int32), pltpu.VMEM(entries, jnp.int32),
+            vmem((levels, srows, block)), vmem((frows, block)),
+            *[pltpu.VMEM(shape, jnp.int32) for shape in tables],
+            *[pltpu.SMEM(shape, jnp.int32) for shape in tables],
             vmem((slots_all, sub, block)), vmem((slots_all, sub, block)),
             vmem((HALVES, slots_all, sub, block)),
             vmem((frows, fanin * block, block)),
@@ -462,13 +511,13 @@
             dma((HALVES * columns * depth,)), dma((HALVES * columns * depth,)),
             dma((HALVES, 2, max(1, depth - 1))), dma((HALVES, 2, max(1, depth - 1))),
             dma((sides,)), dma((sides,)), dma((sides, edges)), dma((sides, edges)),
-            dma((W_PIECES,)),
+            dma((W_PIECES,)), dma((6,)),
         ] + [vmem((srows, sub, block))] * (HALVES + 2 * HALVES * (depth - 1)),
         compiler_params=pltpu.CompilerParams(
-            collective_id=0, has_side_effects=True, vmem_limit_bytes=48 * 2 ** 20),
+            collective_id=0, has_side_effects=True, vmem_limit_bytes=56 * 2 ** 20),
         cost_estimate=pl.CostEstimate(
             flops=6 * levels * frows * fanin * block * block, bytes_accessed=16 * 2 ** 20, transcendentals=0),
-    )(send_rows, pick, source, remap_weights.reshape(frows, fanin * block, block), smoothing)
+    )(intersection_devices.T, intersection_rows.T, source, remap_weights.reshape(frows, fanin * block, block), smoothing)
     return field.reshape(levels, frows, block)
 
 

time: 47 us -> 40.2 us (0.86)
  Pallas kernels: 42.3 us -> 38.4 us
  other arithmetic: 1.55 us -> 0 us
  local copies, waits for them, and re-layouts: 2.76 us -> 1.67 us
    pallas_call x1, Pallas kernels: 42.3 us -> 38.4 us  [shards(): pl.pallas_call(functools.partial(kernel, (along_x, along_y, depth, inner,...]
    add x3 -> x0, other arithmetic: 0.76 us -> none  [the longest x1 0.72 us: shards(): codes = intersection_devices * srows + intersection_rows]
    unnamed x5 -> x1, local copies, waits for them, and re-layouts: 2.38 us -> 1.67 us
    reduce_sum x2 -> x0, other arithmetic: 0.6 us -> none  [the longest x1 0.36 us: shards(): jnp.sum(jnp.where(matched, lats[:, None, None, :], 0), axis=3).reshape(-1)]
where the time goes in v3:
time: 40.2 us; the launch traced here: 40 us
  Pallas kernels  38.4 us (96%)
  local copies, waits for them, and re-layouts  1.67 us (4%)
    pallas_call x1, Pallas kernels, shards(): pl.pallas_call(functools.partial(kernel, (along_x, along_y, depth, inner,...  38.4 us
    unnamed x1, local copies, waits for them, and re-layouts  1.67 us

profile of v3, /device:TPU:0, one launch (start us, length us, event | category | flops | bytes accessed | tf_op | source)
XLA Modules:
  0.0 40.0 jit_solution(2395760757463926389)
XLA Ops:
  0.0 38.4 %shard_map.55 = f32[512,128]{1,0:T(8,128)} custom-call(s32[4,512]{1,0:T(4,128)} %bitcast.6, s32[4,512]{1,0:T(4,128)} %bitcast.7, f32[16,32,128]{2,1,0:T(8,128)} %src_in.1, f32[32,512,128]{2,1,0:T(8,128)} %bitcast.4, f32[32,128]{1,0:T(8,128)} %smooth_in.1), custom_call_target="tpu_custom_call" | custom-call | flops 201326592 | bytes 16777216 | tf_op jit(solution)/shard_map/pallas_call | solution.py:492
  38.4 1.7 %copy.7 = f32[16,32,128]{2,1,0:T(8,128)} copy(f32[16,32,128]{2,1,0:T(8,128)} %bitcast.5) | data formatting | bytes 524288

commit v4 on v3

--- a/solution.py
+++ b/solution.py
@@ -26,7 +26,7 @@
     return 1, along_y
 
 
-def kernel(dims, devices_in, rows_in, src_in, weights, smooth_in, out, devices, lat, src, smooth,
+def kernel(dims, devices_in, rows_in, src_in, weights, smooth_in, out, change, devices, lat, src, smooth,
            table_v, pick_v, table, pick, inbox_0, inbox_1, outbox, w_full, w_high, w_low,
            main_a, main_b, side_a, side_b, s_main, s_side, s_in, edge, edge_in,
            send_sem, recv_sem, chain_send, chain_recv, s_send, s_recv, h_send, h_recv, w_sem, in_sem, *chunks):
@@ -119,7 +119,8 @@
     groups_in_tile = LANES // frows
     slot = lax.broadcasted_iota(jnp.int32, (capacity, LANES), 0).astype(jnp.float32)
     mine = lax.broadcasted_iota(jnp.int32, (max(8, depth), LANES), 0) * inner + x * along_y + yi
-    rows_of = jnp.zeros((depth * capacity, LANES), jnp.float32)
+    rows_of = jnp.zeros(table_v.shape, jnp.float32)
+    spare = table_v.shape[1] - depth * capacity
     for n in range(devices.shape[1] // LANES):
         span = slice(n * LANES, (n + 1) * LANES)
         hits = [jnp.where(devices[k:k + 1, span] == mine, 1.0, 0.0) for k in range(fan)]
@@ -131,24 +132,19 @@
                 rank = jnp.where(hits[k][t:t + 1] > 0.5, found[k][t:t + 1], -1.0)
                 part = part + jnp.where(rank == slot, lat[k:k + 1, span].astype(jnp.float32), 0.0)
             parts.append(part)
-        gather = jnp.where(from_lane // frows + n * groups_in_tile == to_lane, 1.0, 0.0).astype(jnp.bfloat16)
-        rows_of = rows_of + count(jnp.concatenate(parts, axis=0) if depth > 1 else parts[0], gather)
+        if spare:
+            parts.append(jnp.zeros((spare, LANES), jnp.float32))
+        owner = lax.broadcasted_iota(jnp.int32, (table_v.shape[0], LANES), 0)
+        lane_of = lax.broadcasted_iota(jnp.int32, (table_v.shape[0], LANES), 1)
+        gather = jnp.where(lane_of // frows + n * groups_in_tile == owner, 1.0, 0.0).astype(jnp.bfloat16)
+        rows_of = rows_of + lax.dot_general(
+            gather, jnp.concatenate(parts, axis=0).astype(jnp.bfloat16), (((1,), (1,)), ((), ())),
+            preferred_element_type=jnp.float32)
     table_v[...] = jnp.clip(rows_of.astype(jnp.int32), 0, srows - 1)
 
-    span = pl.ds(pl.multiple_of(me // groups_in_tile * LANES, LANES), LANES)
-    every = lax.broadcasted_iota(jnp.int32, (along_x * along_y, LANES), 0)
-    named = [devices[k:k + 1, span] for k in range(fan)]
-    hits = [jnp.where(named[k] == every, 1.0, 0.0) for k in range(fan)]
-    found = ranks(hits)
-    for k in range(fan):
-        rank = jnp.sum(hits[k] * found[k], axis=0, keepdims=True).astype(jnp.int32)
-        tile_y = lax.rem(named[k], along_y)
-        base = (named[k] // along_y * inner + lax.rem(tile_y, inner)) * depth + tile_y // inner
-        pick_v[k:k + 1, :] = jnp.clip(base * capacity + rank, 0, columns * depth * capacity - 1)
-    tables = [pltpu.make_async_copy(a, b, in_sem.at[4 + n]) for n, (a, b) in enumerate((
-        (table_v, table), (pick_v, pick)))]
-    for copy in tables:
-        copy.start()
+    table_copy = pltpu.make_async_copy(table_v, table, in_sem.at[4])
+    table_copy.start()
+    pick_copy = pltpu.make_async_copy(pick_v, pick, in_sem.at[5])
     my_lane = lax.rem(me, groups_in_tile) * frows
     loads[0].wait()
 
@@ -162,8 +158,7 @@
             own[0][place, l, :] = jnp.where(lane_8 < width, low, swapped(high))
             own[1][place, l, :] = jnp.where(lane_8 < width, swapped(low), high)
 
-    for copy in tables:
-        copy.wait()
+    table_copy.wait()
     pl.semaphore_wait(barrier, total)
 
     def chain_copy(h, up, t):
@@ -186,7 +181,7 @@
         def fill(c, write):
             owner = c // inner * along_y + z * inner + lax.rem(c, inner)
             for j in range(capacity):
-                write((c * depth + tile) * capacity + j, chunk[table[tile * capacity + j, owner]])
+                write((c * depth + tile) * capacity + j, chunk[table[owner, tile * capacity + j]])
 
         def to_outbox(n, value):
             outbox[h, n] = value
@@ -312,6 +307,18 @@
             else:
                 edge_in[k] = jnp.zeros(edge_in.shape[1:], jnp.float32)
 
+    span = pl.ds(pl.multiple_of(me // groups_in_tile * LANES, LANES), LANES)
+    every = lax.broadcasted_iota(jnp.int32, (along_x * along_y, LANES), 0)
+    named = [devices[k:k + 1, span] for k in range(fan)]
+    hits = [jnp.where(named[k] == every, 1.0, 0.0) for k in range(fan)]
+    found = ranks(hits)
+    for k in range(fan):
+        rank = jnp.sum(hits[k] * found[k], axis=0, keepdims=True).astype(jnp.int32)
+        tile_y = lax.rem(named[k], along_y)
+        base = (named[k] // along_y * inner + lax.rem(tile_y, inner)) * depth + tile_y // inner
+        pick_v[k:k + 1, :] = jnp.clip(base * capacity + rank, 0, columns * depth * capacity - 1)
+    pick_copy.start()
+
     done = 0
     events = sorted((t + 1.5 * h, h, t) for h in range(HALVES) for t in range(depth - 1))
     for n, (_, h, t) in enumerate(events):
@@ -348,6 +355,7 @@
         s_side[high] = side(s_in[at[1, -1], i:i + 1, :], s_in[at[1, 1], i:i + 1, :])
 
     landed(0)
+    pick_copy.wait()
     products(0, 0, groups)
     landed(1)
 
@@ -437,18 +445,20 @@
                + jnp.where(first, h_up, u_up) - 4.0 * u)
         lap_h = (sides[r + 1] + sides[r - 1] + jnp.where(last, u_down, h_down)
                  + jnp.where(first, u_up, h_up) - 4.0 * h)
-        write(r, u + s_main[r] * lap, h + s_side[r] * lap_h)
-
-    def write_b(r, u, h):
-        main_b[r] = u
+        write(r, u, s_main[r] * lap, h + s_side[r] * lap_h)
+
+    def write_b(r, u, step, h):
+        main_b[r] = u + step
         side_b[r] = h
 
-    def write_a(r, u, h):
-        main_a[r] = u
+    def write_a(r, u, step, h):
+        main_a[r] = u + step
         side_a[r] = h
 
-    def write_out(r, u, h):
-        out[pl.ds(r - PASSES, levels, stride=frows), :] = u
+    def write_out(r, u, step, h):
+        place = pl.ds(r - PASSES, levels, stride=frows)
+        out[place, :] = u
+        change[place, :] = step
 
     for p, (main, sides, write) in enumerate((
             (main_a, side_a, write_b), (main_b, side_b, write_a), (main_a, side_a, write_out))):
@@ -483,17 +493,17 @@
     in_vmem = pl.BlockSpec(memory_space=pltpu.VMEM)
     anywhere = pl.BlockSpec(memory_space=pl.ANY)
     entries = (fanin, intersection_devices.shape[0])
-    tables = ((depth * capacity, block), (fanin, block))
+    tables = ((devices, -(-depth * capacity // block) * block), (fanin, block))
     slots_all = columns * depth * capacity
     dma = pltpu.SemaphoreType.DMA
     sides = len(DIRS)
     edges = frows // PER_TILE
     halves = pltpu.VMEM((HALVES, frows, fanin * block // HALVES, block), jnp.bfloat16)
-    field = pl.pallas_call(
+    field, change = pl.pallas_call(
         functools.partial(kernel, (along_x, along_y, depth, inner, capacity)),
-        out_shape=jax.ShapeDtypeStruct((levels * frows, block), jnp.float32),
+        out_shape=[jax.ShapeDtypeStruct((levels * frows, block), jnp.float32)] * 2,
         in_specs=[anywhere] * 5,
-        out_specs=in_vmem,
+        out_specs=[in_vmem] * 2,
         scratch_shapes=[
             pltpu.VMEM(entries, jnp.int32), pltpu.VMEM(entries, jnp.int32),
             vmem((levels, srows, block)), vmem((frows, block)),
@@ -518,7 +528,7 @@
         cost_estimate=pl.CostEstimate(
             flops=6 * levels * frows * fanin * block * block, bytes_accessed=16 * 2 ** 20, transcendentals=0),
     )(intersection_devices.T, intersection_rows.T, source, remap_weights.reshape(frows, fanin * block, block), smoothing)
-    return field.reshape(levels, frows, block)
+    return (field + change).reshape(levels, frows, block)
 
 
 def solution(mesh):

time: 40.2 us -> 40 us (level)
  other arithmetic: 0 us -> 1.76 us
  local copies, waits for them, and re-layouts: 1.67 us -> 0 us
    add x0 -> x1, other arithmetic: none -> 1.76 us  [shards(): return (field + change).reshape(levels, frows, block)]
    unnamed x1 -> x0, local copies, waits for them, and re-layouts: 1.67 us -> none
where the time goes in v4:
time: 40 us; the launch traced here: 39.9 us
  Pallas kernels  38.1 us (95%)
  other arithmetic  1.76 us (4%)
    pallas_call x1, Pallas kernels, shards(): pl.pallas_call(functools.partial(kernel, (along_x, along_y, depth, inner,...  38.1 us
    add x1, other arithmetic, shards(): return (field + change).reshape(levels, frows, block)  1.76 us

profile of v4, /device:TPU:0, one launch (start us, length us, event | category | flops | bytes accessed | tf_op | source)
XLA Modules:
  0.0 39.9 jit_solution(2097405517622999068)
XLA Ops:
  0.0 38.1 %shard_map.55 = (f32[512,128]{1,0:T(8,128)}, f32[512,128]{1,0:T(8,128)}) custom-call(s32[4,512]{1,0:T(4,128)} %bitcast.5, s32[4,512]{1,0:T(4,128)} %bitcast.6, f32[16,32,128]{2,1,0:T(8,128)} %src_in.1, f32[32,512,128]{2,1,0:T(8,128)} %bitcast.4, f32[32,128]{1,0:T(8,128)} %smooth_in.1), custom_call_target="tpu_custom_call" | custom-call | flops 201326592 | bytes 16777216 | tf_op jit(solution)/shard_map/pallas_call | solution.py:502
  38.1 1.8 %add.3 = f32[512,128]{1,0:T(8,128)} add(f32[512,128]{1,0:T(8,128)} %get-tuple-element.7, f32[512,128]{1,0:T(8,128)} %get-tuple-element.8) | non-fusion elementwise | flops 65536 | bytes 786432 | tf_op jit(solution)/shard_map/add | solution.py:531

commit v5 on v4

--- a/solution.py
+++ b/solution.py
@@ -26,7 +26,7 @@
     return 1, along_y
 
 
-def kernel(dims, devices_in, rows_in, src_in, weights, smooth_in, out, change, devices, lat, src, smooth,
+def kernel(dims, devices_in, rows_in, src_in, weights, smooth_in, out, devices, lat, src, smooth,
            table_v, pick_v, table, pick, inbox_0, inbox_1, outbox, w_full, w_high, w_low,
            main_a, main_b, side_a, side_b, s_main, s_side, s_in, edge, edge_in,
            send_sem, recv_sem, chain_send, chain_recv, s_send, s_recv, h_send, h_recv, w_sem, in_sem, *chunks):
@@ -189,7 +189,8 @@
         def to_inbox(n, value):
             inboxes[h][n] = value
 
-        def peer(q, carry):
+        def peer(n, carry):
+            q = jnp.where(lev % 2 == 0, n, columns - n)
             fill(lax.rem(column + q, columns), to_outbox)
             slot_copy(h, q, tile).start()
             return carry
@@ -456,9 +457,7 @@
         side_a[r] = h
 
     def write_out(r, u, step, h):
-        place = pl.ds(r - PASSES, levels, stride=frows)
-        out[place, :] = u
-        change[place, :] = step
+        out[pl.ds(r - PASSES, levels, stride=frows), :] = u + step
 
     for p, (main, sides, write) in enumerate((
             (main_a, side_a, write_b), (main_b, side_b, write_a), (main_a, side_a, write_out))):
@@ -499,11 +498,11 @@
     sides = len(DIRS)
     edges = frows // PER_TILE
     halves = pltpu.VMEM((HALVES, frows, fanin * block // HALVES, block), jnp.bfloat16)
-    field, change = pl.pallas_call(
+    field = pl.pallas_call(
         functools.partial(kernel, (along_x, along_y, depth, inner, capacity)),
-        out_shape=[jax.ShapeDtypeStruct((levels * frows, block), jnp.float32)] * 2,
+        out_shape=jax.ShapeDtypeStruct((levels * frows, block), jnp.float32),
         in_specs=[anywhere] * 5,
-        out_specs=[in_vmem] * 2,
+        out_specs=in_vmem,
         scratch_shapes=[
             pltpu.VMEM(entries, jnp.int32), pltpu.VMEM(entries, jnp.int32),
             vmem((levels, srows, block)), vmem((frows, block)),
@@ -528,7 +527,7 @@
         cost_estimate=pl.CostEstimate(
             flops=6 * levels * frows * fanin * block * block, bytes_accessed=16 * 2 ** 20, transcendentals=0),
     )(intersection_devices.T, intersection_rows.T, source, remap_weights.reshape(frows, fanin * block, block), smoothing)
-    return (field + change).reshape(levels, frows, block)
+    return field.reshape(levels, frows, block)
 
 
 def solution(mesh):

time: 40 us -> 39.8 us (level)
  other arithmetic: 1.76 us -> 0 us
  local copies, waits for them, and re-layouts: 0 us -> 1.67 us
    add x1 -> x0, other arithmetic: 1.76 us -> none  [shards(): return (field + change).reshape(levels, frows, block)]
    unnamed x0 -> x1, local copies, waits for them, and re-layouts: none -> 1.67 us
where the time goes in v5:
time: 39.8 us; the launch traced here: 39.7 us
  Pallas kernels  38 us (95%)
  local copies, waits for them, and re-layouts  1.67 us (4%)
    pallas_call x1, Pallas kernels, shards(): pl.pallas_call(functools.partial(kernel, (along_x, along_y, depth, inner,...  38 us
    unnamed x1, local copies, waits for them, and re-layouts  1.67 us

profile of v5, /device:TPU:0, one launch (start us, length us, event | category | flops | bytes accessed | tf_op | source)
XLA Modules:
  0.0 39.7 jit_solution(15428873709991315088)
XLA Ops:
  0.0 38.0 %shard_map.55 = f32[512,128]{1,0:T(8,128)} custom-call(s32[4,512]{1,0:T(4,128)} %bitcast.6, s32[4,512]{1,0:T(4,128)} %bitcast.7, f32[16,32,128]{2,1,0:T(8,128)} %src_in.1, f32[32,512,128]{2,1,0:T(8,128)} %bitcast.4, f32[32,128]{1,0:T(8,128)} %smooth_in.1), custom_call_target="tpu_custom_call" | custom-call | flops 201326592 | bytes 16777216 | tf_op jit(solution)/shard_map/pallas_call | solution.py:501
  38.0 1.7 %copy.7 = f32[16,32,128]{2,1,0:T(8,128)} copy(f32[16,32,128]{2,1,0:T(8,128)} %bitcast.5) | data formatting | bytes 524288

commit v6 on v5

--- a/solution.py
+++ b/solution.py
@@ -287,6 +287,7 @@
         lax.fori_loop(depth, columns * depth, one, 0)
 
     start_chain(0)
+    start_chain(1)
     ship(0, own[0], z)
     ship(1, own[1], z)
     for k in range(len(DIRS)):
@@ -321,11 +322,9 @@
     pick_copy.start()
 
     done = 0
-    events = sorted((t + 1.5 * h, h, t) for h in range(HALVES) for t in range(depth - 1))
-    for n, (_, h, t) in enumerate(events):
+    events = sorted((t + 0.5 * h, h, t) for h in range(HALVES) for t in range(depth - 1))
+    for _, h, t in events:
         pass_on(h, t)
-        if n == 0:
-            start_chain(1)
         if done < W_PIECES:
             split_weights(done)
             done += 1

time: 39.8 us -> 39.4 us (0.990)
  Pallas kernels: 38 us -> 37.6 us
    pallas_call x1, Pallas kernels: 38 us -> 37.6 us  [shards(): pl.pallas_call(functools.partial(kernel, (along_x, along_y, depth, inner,...]
where the time goes in v6:
time: 39.4 us; the launch traced here: 39.3 us
  Pallas kernels  37.6 us (95%)
  local copies, waits for them, and re-layouts  1.67 us (4%)
    pallas_call x1, Pallas kernels, shards(): pl.pallas_call(functools.partial(kernel, (along_x, along_y, depth, inner,...  37.6 us
    unnamed x1, local copies, waits for them, and re-layouts  1.67 us

profile of v6, /device:TPU:0, one launch (start us, length us, event | category | flops | bytes accessed | tf_op | source)
XLA Modules:
  0.0 39.3 jit_solution(1378601459583585561)
XLA Ops:
  0.0 37.6 %shard_map.55 = f32[512,128]{1,0:T(8,128)} custom-call(s32[4,512]{1,0:T(4,128)} %bitcast.6, s32[4,512]{1,0:T(4,128)} %bitcast.7, f32[16,32,128]{2,1,0:T(8,128)} %src_in.1, f32[32,512,128]{2,1,0:T(8,128)} %bitcast.4, f32[32,128]{1,0:T(8,128)} %smooth_in.1), custom_call_target="tpu_custom_call" | custom-call | flops 201326592 | bytes 16777216 | tf_op jit(solution)/shard_map/pallas_call | solution.py:500
  37.6 1.7 %copy.7 = f32[16,32,128]{2,1,0:T(8,128)} copy(f32[16,32,128]{2,1,0:T(8,128)} %bitcast.5) | data formatting | bytes 524288
